TPU v7x, 32 devices: a whole 2x2x4 slice. The times are simulated.
32 devices in a mesh: groups: 2 (over x), owner: 2 (over core), tensor: 8 (over z, y).
Axes of the slice: x: 2, y: 2, z: 4, core: 2. Of those that a mesh axis runs over, the one named last changes fastest.
Arguments:
- hidden: bfloat16 [3072, 8192], P(('groups', 'owner'), 'tensor'), parts along dimension 0, may hold values from -6 to 6
- channel_smooth_scale: float32 [8192], P('tensor'), may hold values from 0.3 to 3
- weight: bfloat16 [8192, 8192], P('tensor'), may hold values from -0.09375 to 0.09375
- shrink_matrix_bank: bfloat16 [128, 64, 8192], P(('groups', 'owner'), None, 'tensor'), parts along dimension 0, may hold values from -0.0625 to 0.0625
- expand_matrix_bank: bfloat16 [128, 64, 8192], P(('groups', 'owner'), None, 'tensor'), parts along dimension 0, may hold values from -0.75 to 0.75
- row_adapter_index: int32 [3072, 1], P(('groups', 'owner')), parts along dimension 0, may hold values from 0 to 63; in each aligned block of 768 rows (0 to 767, 768 to 1535, ...) at most 30 rows name the same one
- adapter_storage_slot: int32 [128], P('groups'), parts along dimension 0, may hold values from 0 to 63, each once
Outputs:
- output: bfloat16 [3072, 8192], P(('groups', 'owner'), 'tensor'), parts along dimension 0
There are 2 independent parts, one for each index of `groups`. A program takes and returns all parts, laid end to end along the dimension named above; an argument that names none is the same for every part. Nothing has to cross between parts.
Inputs may be any that keep to these rules, and one draw needn't show every extreme that they name: `row_adapter_index`: among the rows of one owner index (aligned blocks of 768 rows) no adapter is named by more than 30 rows, a bound that some block reaches. `adapter_storage_slot`: A permutation: every storage slot holds one adapter.
All inputs are finite; a program needn't handle non-finite values.
Results may differ from a plain program's by a relative error of at most 0.0049.
Values may be sent and summed in bfloat16 or wider, within the bound.
No kernel may reach another device: no remote copies, remote signals or barrier semaphores. Data moves between devices by JAX's collectives and lax.ppermute only.
A program may use at most 192 MiB of HBM per device.

v0:
```python
import jax
import jax.numpy as jnp
from jax import lax
from jax.sharding import PartitionSpec as P


def slot_rows(row_adapter_index, adapter_storage_slot, segment):
    adapters = adapter_storage_slot.shape[0]
    column_ids = lax.broadcasted_iota(jnp.int32, (1, adapters), 1)
    picked = (row_adapter_index == column_ids).astype(jnp.int32)
    slot_of = jnp.sum(picked * adapter_storage_slot[None, :], axis=1)
    in_slot = (slot_of[:, None] == column_ids).astype(jnp.int32)
    before = jnp.cumsum(in_slot, axis=0) - in_slot
    position = jnp.sum(before * in_slot, axis=1)
    return slot_of * segment + position


def base_columns(smoothed, weight):
    partial_value = jnp.dot(smoothed, weight, preferred_element_type=jnp.float32)
    return lax.psum_scatter(partial_value, "tensor", scatter_dimension=1, tiled=True)


def apply_low_rank_adapter(partial_pieces, row_down_matrices, row_up_matrices):
    partial_value = jnp.einsum(
        "...akd,ard->...akr", partial_pieces, row_down_matrices, preferred_element_type=jnp.float32
    )
    shrunk = lax.psum(partial_value, "tensor").astype(jnp.bfloat16)
    return jnp.einsum(
        "...akr,ard->...akd", shrunk, row_up_matrices, preferred_element_type=jnp.float32
    ).astype(jnp.bfloat16)


def shards(
    hidden,
    channel_smooth_scale,
    weight,
    shrink_matrix_bank,
    expand_matrix_bank,
    row_adapter_index,
    adapter_storage_slot,
):
    row_count, width_local = hidden.shape
    owners = lax.axis_size("owner")
    adapters = adapter_storage_slot.shape[0]
    resident_adapters = shrink_matrix_bank.shape[0]
    segment = 5 * row_count // (2 * adapters)
    flat_index = slot_rows(row_adapter_index, adapter_storage_slot, segment)
    smoothed = (hidden.astype(jnp.float32) / channel_smooth_scale).astype(jnp.bfloat16)
    buffer = jnp.zeros((adapters * segment, width_local), jnp.bfloat16).at[flat_index].set(hidden)
    base_sum = base_columns(smoothed, weight)
    sending = buffer.reshape(owners, resident_adapters, segment, width_local)
    replied_rows = apply_low_rank_adapter(
        lax.all_to_all(sending, "owner", split_axis=0, concat_axis=0, tiled=True),
        shrink_matrix_bank,
        expand_matrix_bank,
    )
    slotted = lax.all_to_all(
        replied_rows, "owner", split_axis=0, concat_axis=0, tiled=True
    ).reshape(adapters * segment, width_local)
    row_deltas = slotted[flat_index]
    return (base_sum + 0.5 * row_deltas.astype(jnp.float32)).astype(jnp.bfloat16)


def solution(mesh):
    placed = (
        P(("groups", "owner"), "tensor"),
        P("tensor"),
        P("tensor", None),
        P(("groups", "owner"), None, "tensor"),
        P(("groups", "owner"), None, "tensor"),
        P(("groups", "owner"), None),
        P("groups"),
    )
    return jax.shard_map(
        shards,
        mesh=mesh,
        in_specs=placed,
        out_specs=P(("groups", "owner"), "tensor"),
        check_vma=False,
    )
```

profile of v0, /device:TPU:0, one launch (start us, length us, event | category | flops | bytes accessed | tf_op | source)
XLA Modules:
  0.0 464.4 jit_solution(8576446859151773129)
XLA Ops:
  6.5 0.0 reduce-scatter.2.cloned.1.call-start
  6.5 21.6 %fusion.9 = f32[768,8192]{1,0:T(8,128)} fusion(bf16[1024,8192]{1,0:T(8,128)(2,1)} %param.9, bf16[768,1024]{1,0:T(8,128)(2,1)} %param.7, f32[1024]{0:T(1024)} %param.8), kind=kOutput, calls=%fused_computation.12 | convolution fusion | flops 12887261184 | bytes 43520000 | tf_op jit(solution)/shard_map/dot_general | solution.py:19
  28.1 0.0 reduce-scatter.2.cloned.1.call-update
  28.2 0.7 copy-done
  28.8 0.0 copy-done.1
  28.8 0.1 select_reduce_fusion
  29.0 1.8 reduce-window.6
  30.8 0.3 slice_reduce_fusion
  31.1 0.1 fusion.19
  31.3 8.9 %scatter_custom_fusion = bf16[1920,1024]{1,0:T(8,128)(2,1)} fusion(s32[768]{0:T(1024)S(1)} %fusion.21, bf16[768,1024]{1,0:T(8,128)(2,1)} %param.7, bf16[]{:T(256)} %constant.5.clone.1), kind=kCustom, calls=%fused_computation.10 | custom fusion | bytes 3932672 | tf_op jit(solution)/shard_map/scatter | solution.py:49
  40.1 6.0 %reshape.51 = bf16[2,32,30,1024]{3,2,1,0:T(8,128)(2,1)} reshape(bf16[1920,1024]{1,0:T(8,128)(2,1)} %scatter_custom_fusion) | data formatting | bytes 7864320 | tf_op jit(solution)/shard_map/reshape | solution.py:51
  46.2 4.4 copy.11
  50.6 0.0 copy-start.2
  50.6 7.2 %all_to_all.10 = bf16[2,32,30,1024]{3,1,2,0:T(8,128)(2,1)S(1)} all-to-all(bf16[2,32,30,1024]{3,1,2,0:T(8,128)(2,1)S(1)} %copy.11), channel_id=1, replica_groups=mesh['groups'=2,'owner'=2,'tensor'=8] {'owner'}, dimensions={0} | all-to-all | bytes 7864320 | tf_op jit(solution)/shard_map/all_to_all | solution.py:53
  57.8 2.7 fusion.11
  60.4 102.4 %all-reduce.1 = bf16[2,32,30,64]{3,2,0,1:T(8,128)(2,1)S(1)} all-reduce(f32[2,32,30,64]{3,2,0,1:T(8,128)S(1)} %fusion.11), channel_id=1, replica_groups=mesh['groups'=2,'owner'=2,'tensor'=8] {'tensor'}, use_global_device_ids=true, to_apply=%region_6.7 | all-reduce | flops 122880 | bytes 737280 | tf_op jit(solution)/shard_map/psum | solution.py:27
  162.9 3.7 convert_bitcast_fusion
  166.6 2.2 copy.13
  168.8 6.9 %all_to_all.11 = bf16[2,32,30,1024]{3,1,2,0:T(8,128)(2,1)S(1)} all-to-all(bf16[2,32,30,1024]{3,1,2,0:T(8,128)(2,1)S(1)} %copy.13), channel_id=1, replica_groups=mesh['groups'=2,'owner'=2,'tensor'=8] {'owner'}, dimensions={0} | all-to-all | bytes 7864320 | tf_op jit(solution)/shard_map/all_to_all | solution.py:57
  175.7 4.2 copy.14
  179.8 6.1 %reshape.52 = bf16[1920,1024]{1,0:T(8,128)(2,1)} reshape(bf16[2,32,30,1024]{3,2,1,0:T(8,128)(2,1)} %copy.14) | data formatting | bytes 7864320 | tf_op jit(solution)/shard_map/reshape | solution.py:59
  186.0 6.4 %gather_fusion = bf16[768,1024]{1,0:T(8,128)(2,1)S(1)} fusion(bf16[1920,1024]{1,0:T(8,128)(2,1)} %reshape.52, s32[1024]{0:T(1024)S(1)} %pad_clamp_fusion), kind=kCustom, calls=%fused_computation | custom fusion | bytes 3148800 | tf_op jit(solution)/shard_map/gather | solution.py:60
  192.4 261.6 %reduce-scatter.2.cloned.1.call-done = f32[768,1024]{1,0:T(8,128)} async-done(((f32[768,8192]{1,0:T(8,128)}), f32[768,1024]{1,0:T(8,128)}) %reduce-scatter.2.cloned.1.call-update) | async-done | bytes 3145744 | tf_op jit(solution)/shard_map/reduce_scatter | solution.py:20
  454.0 3.6 add_convert_fusion
  (9 shorter events, 0.1 us)
Async XLA Ops:
  6.5 447.4 %reduce-scatter.2.cloned.1.call-start = ((), (), s32[]{:S(2)}) async-start(), calls=%async_computation.3 | async-start | bytes 28311552 | tf_op jit(solution)/shard_map/reduce_scatter | solution.py:20
  28.1 0.7 copy-start
  28.1 0.7 copy-start.1
  50.6 7.2 %copy-start.2 = (bf16[32,64,1024]{2,1,0:T(8,128)(2,1)S(1)}, bf16[32,64,1024]{2,1,0:T(8,128)(2,1)}, u32[]{:S(2)}) copy-start(bf16[32,64,1024]{2,1,0:T(8,128)(2,1)} %param.10) | copy-start | bytes 12582916
Sparse Core Ops, SparseCore 0:
  28.3 425.6 reduce-scatter.1
where the time goes:
time: 465 us; the launch traced here: 464 us
  waiting for transfers between devices  262 us (56%)
  blocking collectives  116 us (25%)
  local copies, waits for them, and re-layouts  39.2 us (8%)
  matrix products  28 us (6%)
  between operations  13.5 us (3%)
  other arithmetic  5.72 us (1%)
    reduce_scatter x1, waiting for transfers between devices, base_columns(): lax.psum_scatter(partial_value, 'tensor', scatter_dimension=1, tiled=True)  262 us
    psum x1, blocking collectives, apply_low_rank_adapter(): shrunk = lax.psum(partial_value, 'tensor').astype(jnp.bfloat16)  102 us
    dot_general x1, matrix products, base_columns(): jnp.dot(smoothed, weight, preferred_element_type=jnp.float32)  21.6 us
    reshape x2, local copies, waits for them, and re-layouts, shards(): sending = buffer.reshape(owners, resident_adapters, segment, width_local)  10.4 us
  transfers between devices with their start and end apart: 1, of which 1 were waited for; matrix products, arithmetic and copies ran while one was open for 10% of the time, Pallas kernels for 0%

commit v1 on v0

v1 whole, which is shorter than its diff:
```python
import functools

import numpy as np
import jax
import jax.numpy as jnp
from jax import lax
from jax.experimental import pallas as pl
from jax.experimental.pallas import tpu as pltpu
from jax.sharding import PartitionSpec as P

F32 = jnp.float32
BF16 = jnp.bfloat16
VMEM_BYTES = 56 * 2**20
SMALL = pl.CostEstimate(flops=1, bytes_accessed=1, transcendentals=0)


def params():
    return pltpu.CompilerParams(vmem_limit_bytes=VMEM_BYTES)


def line_plan(places):
    order = np.full((places, places), -1, np.int64)
    up = {}
    down = {}
    for z in range(places):
        rest = []
        for s in range(1, places):
            named = []
            if z <= s - 1:
                named.append((up, places - s + z))
            if z >= places - s:
                named.append((down, z - places + s))
            if len(named) == 2 and 2 * z >= places:
                named.reverse()
            for i, (table, chunk) in enumerate(named):
                if i == 0:
                    order[z, s - 1] = chunk
                    table[s, z] = s - 1
                else:
                    rest.append((table, s, chunk))
        order[z, places - 1] = z
        for table, s, chunk in rest:
            slot = int(np.flatnonzero(order[z] < 0)[0])
            assert slot < s
            order[z, slot] = chunk
            table[s, z] = slot
    return order, up, down


def pick(z, table, step, places, values):
    slots = sorted({table[step, p] for p in range(places) if (step, p) in table} & set(range(len(values))))
    result = values[slots[0]]
    for slot in slots[1:]:
        here = jnp.zeros((), jnp.bool_)
        for place in range(places):
            if table.get((step, place)) == slot:
                here = here | (z == place)
        result = jnp.where(here, values[slot], result)
    return result


def opening_body(scalars_ref, hidden_ref, scale_ref, w_ref, *refs):
    rest_ref, away_ref = refs[-2:]
    head = hidden_ref.shape[0] - rest_ref.shape[0]

    @pl.when(pl.program_id(0) == 0)
    def _():
        rest_ref[...] = (hidden_ref[head:].astype(F32) / scale_ref[...]).astype(BF16)

    away_ref[...] = jnp.dot(rest_ref[...], w_ref[...], preferred_element_type=F32).astype(BF16)


def opening(hidden, scale, weight, scalars, column, span, first, after=()):
    rows, depth = hidden.shape
    rest = rows - first
    tile = min(512, span)
    whole = lambda j, s: (0, 0)
    return pl.pallas_call(
        opening_body,
        out_shape=[
            jax.ShapeDtypeStruct((rest, depth), BF16),
            jax.ShapeDtypeStruct((rest, span), BF16),
        ],
        grid_spec=pltpu.PrefetchScalarGridSpec(
            num_scalar_prefetch=1,
            grid=(span // tile,),
            in_specs=[
                pl.BlockSpec((rows, depth), whole),
                pl.BlockSpec((1, depth), whole),
                pl.BlockSpec((depth, tile), lambda j, s: (0, s[column] * (span // tile) + j)),
            ]
            + [pl.BlockSpec(memory_space=pl.ANY)] * len(after),
            out_specs=[
                pl.BlockSpec((rest, depth), whole),
                pl.BlockSpec((rest, tile), lambda j, s: (0, j)),
            ],
        ),
        compiler_params=params(),
        cost_estimate=SMALL,
    )(scalars, hidden, scale.reshape(1, depth), weight, *after)


def product_body(added, scalars_ref, x_ref, w_ref, *refs):
    out_ref = refs[-1]
    total = jnp.dot(x_ref[...], w_ref[...], preferred_element_type=F32)
    for ref in refs[:added]:
        total = total + ref[...].astype(F32)
    out_ref[...] = total.astype(out_ref.dtype)


def sums_body(column, flagged, scalars_ref, sum_ref, *refs):
    got, others, outs = refs[:flagged], refs[flagged : 2 * flagged], refs[-flagged:]
    for i in range(flagged):
        mine = jnp.where(
            scalars_ref[column + 1 + i] != 0, sum_ref[...].astype(F32), others[i][...].astype(F32)
        )
        outs[i][...] = (mine + got[i][...].astype(F32)).astype(BF16)


def sum_body(scalars_ref, sum_ref, got_ref, *refs):
    refs[-1][...] = (sum_ref[...].astype(F32) + got_ref[...].astype(F32)).astype(BF16)


def sums(scalars, column, values, block, got, others=(), after=()):
    rows, width = got[0].shape
    tile = min(512, width)
    one = pl.BlockSpec((rows, tile), lambda j, s: (0, j))
    shape = jax.ShapeDtypeStruct((rows, width), BF16)
    count = len(others)
    return pl.pallas_call(
        functools.partial(sums_body, column, count) if count else sum_body,
        out_shape=[shape] * max(count, 1),
        grid_spec=pltpu.PrefetchScalarGridSpec(
            num_scalar_prefetch=1,
            grid=(width // tile,),
            in_specs=[pl.BlockSpec((rows, tile), lambda j, s: (block, j))]
            + [one] * (len(got) + count)
            + [pl.BlockSpec(memory_space=pl.ANY)] * len(after),
            out_specs=[one] * max(count, 1),
        ),
        compiler_params=params(),
        cost_estimate=SMALL,
    )(scalars, values, *got, *others, *after)


def merge_body(total_ref, got_ref, *refs):
    total_out, sent_out = refs[-2:]
    total = total_ref[...] + got_ref[...].astype(F32)
    total_out[...] = total
    sent_out[...] = total.astype(BF16)


def merge(total, got, after=()):
    block = pl.BlockSpec(total.shape, lambda: (0, 0))
    return pl.pallas_call(
        merge_body,
        out_shape=[jax.ShapeDtypeStruct(total.shape, F32), jax.ShapeDtypeStruct(total.shape, BF16)],
        in_specs=[block, block] + [pl.BlockSpec(memory_space=pl.ANY)] * len(after),
        out_specs=[block, block],
        compiler_params=params(),
        cost_estimate=SMALL,
    )(total, got, *after)


def product(x, weight, scalars, column, span, adds=(), after=(), dtype=BF16, rows=None, block=0, tile=512):
    depth = x.shape[1]
    rows = rows or x.shape[0]
    tile = min(tile, span)
    steps = span // tile
    out_block = pl.BlockSpec((rows, tile), lambda j, s: (0, j))
    size = jnp.dtype(dtype).itemsize
    out_shape = jax.ShapeDtypeStruct((rows, span), dtype)
    return pl.pallas_call(
        functools.partial(product_body, len(adds)),
        out_shape=out_shape,
        grid_spec=pltpu.PrefetchScalarGridSpec(
            num_scalar_prefetch=1,
            grid=(steps,),
            in_specs=[
                pl.BlockSpec((rows, depth), lambda j, s: (block, 0)),
                pl.BlockSpec((depth, tile), lambda j, s: (0, s[column] * steps + j)),
            ]
            + [
                out_block if a.shape[0] == rows else pl.BlockSpec((rows, tile), lambda j, s: (block, j))
                for a in adds
            ]
            + [pl.BlockSpec(memory_space=pl.ANY)] * len(after),
            out_specs=out_block,
        ),
        compiler_params=params(),
        cost_estimate=pl.CostEstimate(
            flops=2 * rows * depth * span,
            bytes_accessed=2 * rows * depth + 2 * depth * span + rows * span * (size + 2 * len(adds)),
            transcendentals=0,
        ),
    )(scalars, x, weight, *adds, *after)


def holds(slot, first, rank):
    lane = lax.broadcasted_iota(jnp.int32, slot.shape, 1)
    return slot == first + lane // rank


def by_half(own_ref, other_ref, use):
    j = pl.program_id(0)
    half = pl.num_programs(0) // 2

    @pl.when(j < half)
    def _():
        use(own_ref[...])

    @pl.when(j >= half)
    def _():
        use(other_ref[...])


def bank_specs(bank, tile):
    half = bank.shape[0] // tile
    return [
        pl.BlockSpec((tile, bank.shape[1]), lambda j: (jnp.minimum(j, half - 1), 0)),
        pl.BlockSpec((tile, bank.shape[1]), lambda j: (jnp.maximum(j - half, 0), 0)),
    ]


def shrink_body(rank, slot_ref, x_ref, own_ref, other_ref, *refs):
    out_ref, total = refs[-2:]
    j = pl.program_id(0)
    lanes = total.shape[1]
    each = own_ref.shape[0] // lanes

    @pl.when(j == 0)
    def _():
        total[...] = jnp.zeros_like(total)

    def use(bank):
        every = lax.dot_general(x_ref[...], bank, (((1,), (1,)), ((), ())), preferred_element_type=F32)
        slot = slot_ref[...]
        kept = total[...]
        for h in range(each):
            mine = holds(slot, (j * each + h) * (lanes // rank), rank)
            kept = kept + jnp.where(mine, every[:, h * lanes : (h + 1) * lanes], 0.0)
        total[...] = kept

    by_half(own_ref, other_ref, use)

    @pl.when(j == pl.num_programs(0) - 1)
    def _():
        both = total[...]
        both = both + pltpu.roll(both, rank, 1)
        half = out_ref.shape[0]
        left = lax.broadcasted_iota(jnp.int32, (half, lanes), 1) < rank
        out_ref[...] = jnp.where(left, both[:half], both[half:])


def shrink_rows(x, own, other, slot, rank, after=()):
    rows, depth = x.shape
    lanes = slot.shape[1]
    tile = min(4 * lanes, own.shape[0])
    return pl.pallas_call(
        functools.partial(shrink_body, rank),
        out_shape=jax.ShapeDtypeStruct((rows // 2, lanes), F32),
        grid=(2 * own.shape[0] // tile,),
        in_specs=[
            pl.BlockSpec((rows, lanes), lambda j: (0, 0)),
            pl.BlockSpec((rows, depth), lambda j: (0, 0)),
        ]
        + bank_specs(own, tile)
        + [pl.BlockSpec(memory_space=pl.ANY)] * len(after),
        out_specs=pl.BlockSpec((rows // 2, lanes), lambda j: (0, 0)),
        scratch_shapes=[pltpu.VMEM((rows, lanes), F32)],
        compiler_params=params(),
        cost_estimate=SMALL,
    )(slot, x, own, other, *after)


def expand_body(rank, slot_ref, shrunk_ref, own_ref, other_ref, rest_ref, *refs):
    out_ref, total, unpacked = refs[-3:]
    j = pl.program_id(0)
    lanes = shrunk_ref.shape[1]
    each = own_ref.shape[0] // lanes

    @pl.when(j == 0)
    def _():
        total[...] = jnp.zeros_like(total)
        packed = shrunk_ref[...].astype(F32)
        half = packed.shape[0]
        left = lax.broadcasted_iota(jnp.int32, packed.shape, 1) < rank
        turned = pltpu.roll(packed, rank, 1)
        unpacked[:half] = jnp.where(left, packed, turned)
        unpacked[half:] = jnp.where(left, turned, packed)

    def use(bank):
        slot = slot_ref[...]
        shrunk = unpacked[...]
        spread = [
            jnp.where(holds(slot, (j * each + h) * (lanes // rank), rank), shrunk, 0.0).astype(BF16)
            for h in range(each)
        ]
        total[...] += jnp.dot(jnp.concatenate(spread, axis=1), bank, preferred_element_type=F32)

    by_half(own_ref, other_ref, use)

    @pl.when(j == pl.num_programs(0) - 1)
    def _():
        delta = 0.5 * total[...].astype(BF16).astype(F32)
        head = delta.shape[0] - rest_ref.shape[0]
        out_ref[:head] = delta[:head]
        out_ref[head:] = rest_ref[...] + delta[head:]


def expand_rows(shrunk, own, other, slot, rank, rest, after=()):
    rows, lanes = slot.shape
    width = own.shape[1]
    tile = min(4 * lanes, own.shape[0])
    whole = lambda j: (0, 0)
    return pl.pallas_call(
        functools.partial(expand_body, rank),
        out_shape=jax.ShapeDtypeStruct((rows, width), F32),
        grid=(2 * own.shape[0] // tile,),
        in_specs=[pl.BlockSpec((rows, lanes), whole), pl.BlockSpec((rows // 2, lanes), whole)]
        + bank_specs(own, tile)
        + [pl.BlockSpec(rest.shape, whole)]
        + [pl.BlockSpec(memory_space=pl.ANY)] * len(after),
        out_specs=pl.BlockSpec((rows, width), whole),
        scratch_shapes=[pltpu.VMEM((rows, width), F32), pltpu.VMEM((rows, lanes), F32)],
        compiler_params=params(),
        cost_estimate=SMALL,
    )(slot, shrunk, own, other, rest, *after)


def finish_body(blocks, base_ref, kept_ref, part_ref, y_ref, *refs):
    ends, out_ref = refs[: 2 * blocks], refs[-1]
    size = ends[0].shape[0]
    head = base_ref.shape[0] - blocks * size
    total = base_ref[:head] + kept_ref[...].astype(F32) + part_ref[...].astype(F32)
    out_ref[:head] = total.astype(out_ref.dtype)
    for b in range(blocks):
        at = slice(head + b * size, head + (b + 1) * size)
        total = base_ref[at] + y_ref[b * size : (b + 1) * size].astype(F32)
        total = total + ends[2 * b][...].astype(F32) + ends[2 * b + 1][...].astype(F32)
        out_ref[at] = total.astype(out_ref.dtype)


def finish(base, kept, part, y_part, ends):
    rows, width = base.shape
    tile = min(width, 512)
    operands = [base, kept, part, y_part] + [end for pair in ends for end in pair]
    return pl.pallas_call(
        functools.partial(finish_body, len(ends)),
        out_shape=jax.ShapeDtypeStruct((rows, width), BF16),
        grid=(width // tile,),
        in_specs=[pl.BlockSpec((a.shape[0], tile), lambda j: (0, j)) for a in operands],
        out_specs=pl.BlockSpec((rows, tile), lambda j: (0, j)),
        compiler_params=params(),
        cost_estimate=SMALL,
    )(*operands)


def shards(
    hidden,
    channel_smooth_scale,
    weight,
    shrink_matrix_bank,
    expand_matrix_bank,
    row_adapter_index,
    adapter_storage_slot,
):
    rows, depth = hidden.shape
    tensors = lax.axis_size("tensor")
    assert lax.axis_size("owner") == 2 and tensors > 4 and tensors.bit_count() == 1
    places = tensors // 2
    width = weight.shape[1] // tensors
    adapters = adapter_storage_slot.shape[0]
    resident, rank, _ = shrink_matrix_bank.shape
    t = lax.axis_index("tensor")
    z, y = t // 2, t % 2
    o = lax.axis_index("owner")
    swap_y = [(i, i ^ 1) for i in range(tensors)]
    swap_owner = [(0, 1), (1, 0)]
    first = rows // 256 * 48
    lines = [list(range(i, tensors, 2)) for i in range(2)]
    order, up, down = line_plan(places)
    final = places - 1
    table = [
        [2 * order[i // 2, k] + 1 - i % 2 for k in range(places)]
        + [
            entry
            for k in range(places)
            for entry in (
                2 * order[i // 2, k] + i % 2,
                up.get((final, i // 2)) == final - 1,
                down.get((final, i // 2)) == final - 1,
            )
        ]
        + [0]
        for i in range(tensors)
    ]
    scalars = lax.dynamic_index_in_dim(jnp.asarray(np.array(table, np.int32)), t, keepdims=False)
    away_at = list(range(places))
    here_at = [places + 3 * k for k in range(places)]
    zero_at = 4 * places

    shrink = shrink_matrix_bank.reshape(resident * rank, depth)
    expand = expand_matrix_bank.reshape(resident * rank, width)
    shrink_other = lax.ppermute(shrink, "owner", swap_owner)
    expand_other = lax.ppermute(expand, "owner", swap_owner)
    names = lax.broadcasted_iota(jnp.int32, (1, adapters), 1)
    slot = jnp.sum(
        (row_adapter_index == names).astype(jnp.int32) * adapter_storage_slot[None, :], axis=1, keepdims=True
    )
    slot = jnp.where(slot < o * resident, slot + adapters, slot) - o * resident
    slot = jnp.broadcast_to(slot, (rows, 2 * rank))

    def send_along_y(k, last):
        sent = product(x_rest, weight, scalars, away_at[k], width, after=(last,))
        y_got.append(lax.ppermute(sent, "tensor", swap_y))
        return sent

    x_first = (hidden[:first].astype(F32) / channel_smooth_scale).astype(BF16)
    z_all = product(x_first, weight, scalars, zero_at, 2 * width * places, tile=2048)

    x_rest, away = opening(
        hidden, channel_smooth_scale, weight, scalars, away_at[0], width, first, after=(z_all,)
    )
    y_got = [lax.ppermute(away, "tensor", swap_y)]
    last = send_along_y(1, away)
    last = part_sum = shrink_rows(
        hidden, shrink, shrink_other, slot, rank, after=(last, expand_other)
    )
    z_sum = lax.psum_scatter(
        z_all, "tensor", scatter_dimension=1, axis_index_groups=lines, tiled=True
    )
    z_sent = jnp.where(y == 0, z_sum[:, width:], z_sum[:, :width])
    z_kept = jnp.where(y == 0, z_sum[:, :width], z_sum[:, width:])
    z_part = lax.ppermute(z_sent, "tensor", swap_y)
    every = lax.all_gather(part_sum, "tensor", axis=0)
    shrunk = jnp.sum(every, axis=0).astype(BF16)

    values = []
    arrived = ()
    for s in range(1, places):
        k = s - 1
        ups = [(a * 2 + i, a * 2 + 2 + i) for a in range(places - 1) for i in range(2) if a <= s - 1]
        downs = [(a * 2 + i, a * 2 - 2 + i) for a in range(1, places) for i in range(2) if a >= places - s]
        last = whole = product(
            x_rest, weight, scalars, here_at[k], width, (y_got[k],), after=(last,)
        )
        if s == 1:
            arrived = (lax.ppermute(last, "tensor", ups + downs),)
        else:
            if 2 * s <= places:
                if len(arrived) == 1:
                    last = whole = sums(scalars, 0, whole, 0, arrived, after=(last,))[0]
                else:
                    whole = whole.astype(F32) + arrived[0].astype(F32) + arrived[1].astype(F32)
                    whole = last = whole.astype(BF16)
                outs = whole, whole
            else:
                got = arrived if len(arrived) == 2 else arrived * 2
                if s < final:
                    outs = [
                        (pick(z, table, s, places, values + [whole]).astype(F32) + one.astype(F32)).astype(BF16)
                        for table, one in zip((up, down), got)
                    ]
                else:
                    others = [pick(z, table, s, places, values) for table in (up, down)]
                    outs = sums(scalars, here_at[k], whole, 0, got, others, after=(last,))
                last = outs[0]
            arrived = lax.ppermute(outs[0], "tensor", ups), lax.ppermute(outs[1], "tensor", downs)
        values.append(whole)
        if s + 1 < places:
            last = send_along_y(s + 1, last)
        if s == 1:
            last = own = product(
                x_rest, weight, scalars, here_at[final], width, after=(last,), dtype=F32
            )

    base = expand_rows(shrunk, expand, expand_other, slot, rank, own, after=(last,))
    return finish(base, z_kept, z_part, y_got[-1], [arrived])


def solution(mesh):
    placed = (
        P(("groups", "owner"), "tensor"),
        P("tensor"),
        P("tensor", None),
        P(("groups", "owner"), None, "tensor"),
        P(("groups", "owner"), None, "tensor"),
        P(("groups", "owner"), None),
        P("groups"),
    )
    return jax.shard_map(
        shards,
        mesh=mesh,
        in_specs=placed,
        out_specs=P(("groups", "owner"), "tensor"),
        check_vma=False,
    )
```

time: 465 us -> 198 us (0.43)
  waiting for transfers between devices: 262 us -> 52.8 us
  blocking collectives: 116 us -> 0 us
  Pallas kernels: 0 us -> 88.1 us
  local copies, waits for them, and re-layouts: 39.2 us -> 7.49 us
  matrix products: 28 us -> 0 us
  starting transfers between devices: 0.01 us -> 27.6 us
    reduce_scatter x1, waiting for transfers between devices: 262 us -> 0.01 us  [shards(): lax.psum_scatter(z_all, 'tensor', scatter_dimension=1, axis_index_groups=...]
    psum x1 -> x0, blocking collectives: 102 us -> none  [apply_low_rank_adapter(): shrunk = lax.psum(partial_value, 'tensor').astype(jnp.bfloat16)]
    pallas_call x0 -> x14, Pallas kernels: none -> 88.1 us  [the longest x8 44.6 us: product(): pl.pallas_call(functools.partial(product_body, len(adds)), out_shape=out_...]
    ppermute x0 -> x12, waiting for transfers between devices: none -> 52.8 us  [the longest x2 16.4 us: shards(): lax.ppermute(outs[0], 'tensor', ups)]
    dot_general x3 -> x0, matrix products: 28 us -> none  [the longest x1 21.6 us: base_columns(): jnp.dot(smoothed, weight, preferred_element_type=jnp.float32)]
    ppermute x0 -> x12, starting transfers between devices: none -> 27.5 us  [the longest x2 13.6 us: shards(): lax.ppermute(outs[0], 'tensor', ups)]
    reshape x3 -> x0, local copies, waits for them, and re-layouts: 16.6 us -> none  [the longest x2 10.4 us: shards(): sending = buffer.reshape(owners, resident_adapters, segment, width_local)]
    all_to_all x2 -> x0, blocking collectives: 14 us -> none  [the longest x1 7.16 us: shards(): lax.all_to_all(sending, 'owner', split_axis=0, concat_axis=0, tiled=True)]
  transfers between devices with their start and end apart: 1 -> 14, of which waited for: 1 -> 6; matrix products, arithmetic and copies ran while one was open for 10% -> 4% of each run, Pallas kernels for 0% -> 43%
where the time goes in v1:
time: 198 us; the launch traced here: 197 us
  Pallas kernels  88.1 us (44%)
  waiting for transfers between devices  52.8 us (27%)
  starting transfers between devices  27.6 us (14%)
  between operations  15 us (8%)
  local copies, waits for them, and re-layouts  7.49 us (4%)
  other arithmetic  5.83 us (3%)
    pallas_call x8, Pallas kernels, product(): pl.pallas_call(functools.partial(product_body, len(adds)), out_shape=out_...  44.6 us
    ppermute x2, waiting for transfers between devices, shards(): lax.ppermute(outs[0], 'tensor', ups)  16.4 us
    ppermute x2, starting transfers between devices, shards(): lax.ppermute(outs[0], 'tensor', ups)  13.6 us
    pallas_call x1, Pallas kernels, expand_rows(): pl.pallas_call(functools.partial(expand_body, rank), out_shape=jax.ShapeD...  13.6 us
    ppermute x1, waiting for transfers between devices, shards(): arrived = (lax.ppermute(last, 'tensor', ups + downs),)  13.5 us
    pallas_call x1, Pallas kernels, shrink_rows(): pl.pallas_call(functools.partial(shrink_body, rank), out_shape=jax.ShapeD...  12 us
    ppermute x1, waiting for transfers between devices, shards(): y_got = [lax.ppermute(away, 'tensor', swap_y)]  10.9 us
    pallas_call x2, Pallas kernels, sums(): pl.pallas_call(functools.partial(sums_body, column, count) if count else...  8.36 us
  transfers between devices with their start and end apart: 14, of which 6 were waited for; matrix products, arithmetic and copies ran while one was open for 4% of the time, Pallas kernels for 43%

profile of v1, /device:TPU:0, one launch (start us, length us, event | category | flops | bytes accessed | tf_op | source)
XLA Modules:
  0.0 196.8 jit_solution(16734120505617928171)
XLA Ops:
  10.9 9.4 %shard_map.82.refs_0_ = bf16[144,8192]{1,0:T(8,128)(2,1)} custom-call(s32[17]{0:T(128)} %dynamic-slice_bitcast_fusion.scalars_ref, bf16[144,1024]{1,0:T(8,128)(2,1)} %divide_convert_fusion.x_ref, bf16[1024,8192]{1,0:T(8,128)(2,1)} %w_ref.17), custom_call_target="tpu_custom_call" | custom-call | flops 2415919104 | bytes 19431424 | tf_op jit(solution)/shard_map/pallas_call | solution.py:173
  20.3 5.2 %shard_map.83 = (bf16[624,1024]{1,0:T(8,128)(2,1)}, bf16[624,1024]{1,0:T(8,128)(2,1)}) custom-call(s32[17]{0:T(128)} %dynamic-slice_bitcast_fusion.scalars_ref, bf16[768,1024]{1,0:T(8,128)(2,1)} %x_ref.1, f32[1,1024]{1,0:T(1,128)} %bitcast.11, bf16[1024,8192]{1,0:T(8,128)(2,1)} %w_ref.17, bf16[144,8192]{1,0:T(8,128)(2,1)} %shard_map.82.refs_0_), custom_call_target="tpu_custom_call" | custom-call | flops 1 | bytes 1 | tf_op jit(solution)/shard_map/pallas_call | solution.py:78
  25.5 3.0 %collective-permute-start.2 = (bf16[624,1024]{1,0:T(8,128)(2,1)}, bf16[624,1024]{1,0:T(8,128)(2,1)S(1)}, u32[]{:S(2)}, u32[]{:S(2)}) collective-permute-start(bf16[624,1024]{1,0:T(8,128)(2,1)} %get-tuple-element.10.refs_0_), channel_id=1, source_target_pairs={{0,1},{1,0},{2,3},{3,2},{4,5},{5,4},{6,7},{7,6},{8,9},{9,8},{10,11... | collective-permute-start | bytes 3833864 | tf_op jit(solution)/shard_map/ppermute | solution.py:425
  28.5 5.0 %shard_map.84.refs_0_ = bf16[624,1024]{1,0:T(8,128)(2,1)} custom-call(s32[17]{0:T(128)} %dynamic-slice_bitcast_fusion.scalars_ref, bf16[624,1024]{1,0:T(8,128)(2,1)} %get-tuple-element.9.x_ref, bf16[1024,8192]{1,0:T(8,128)(2,1)} %w_ref.17, bf16[624,1024]{1,0:T(8,128)(2,1)} %get-tuple-element.10.refs_0_), custom_call_target="tpu_custom_call" | custom-call | flops 1308622848 | bytes 4653056 | tf_op jit(solution)/shard_map/pallas_call | solution.py:173
  34.7 12.0 %shard_map.85.refs_1_ = f32[384,128]{1,0:T(8,128)} custom-call(s32[768,128]{1,0:T(8,128)} %broadcast_in_dim.2.slot_ref, bf16[768,1024]{1,0:T(8,128)(2,1)} %x_ref.1, bf16[2048,1024]{1,0:T(8,128)(2,1)} %bitcast.7, bf16[2048,1024]{1,0:T(8,128)(2,1)} %collective-permute-done.other_ref, bf16[624,1024]{1,0:T(8,128)(2,1)} %shard_map.84.refs_0_, ...), custom_call_target="tpu_custom_call" | custom-call | flops 1 | bytes 1 | tf_op jit(solution)/shard_map/pallas_call | solution.py:259
  46.7 10.9 %collective-permute-done.2.refs_0_ = bf16[624,1024]{1,0:T(8,128)(2,1)S(1)} collective-permute-done((bf16[624,1024]{1,0:T(8,128)(2,1)}, bf16[624,1024]{1,0:T(8,128)(2,1)S(1)}, u32[]{:S(2)}, u32[]{:S(2)}) %collective-permute-start.2) | collective-permute-done | bytes 1277984 | tf_op jit(solution)/shard_map/ppermute | solution.py:425
  58.7 5.1 %shard_map.86.refs_0_.refs_2_.refs_3_ = bf16[624,1024]{1,0:T(8,128)(2,1)} custom-call(s32[17]{0:T(128)} %dynamic-slice_bitcast_fusion.scalars_ref, bf16[624,1024]{1,0:T(8,128)(2,1)} %get-tuple-element.9.x_ref, bf16[1024,8192]{1,0:T(8,128)(2,1)} %w_ref.17, bf16[624,1024]{1,0:T(8,128)(2,1)} %copy-done.1, f32[384,128]{1,0:T(8,128)} %shard_map.85.refs_1_), custom_call_target="tpu_custom_call" | custom-call | flops 1308622848 | bytes 5931008 | tf_op jit(solution)/shard_map/pallas_call | solution.py:173
  63.8 4.2 %collective-permute-start.5 = (bf16[624,1024]{1,0:T(8,128)(2,1)}, bf16[624,1024]{1,0:T(8,128)(2,1)S(1)}, u32[]{:S(2)}, u32[]{:S(2)}) collective-permute-start(bf16[624,1024]{1,0:T(8,128)(2,1)} %shard_map.86.refs_0_.refs_2_.refs_3_), channel_id=1, source_target_pairs={{0,2},{1,3},{6,4},{7,5},{8,10},{9,11},{14,12},{15,13},{16,18},{17,... | collective-permute-start | bytes 3833864 | tf_op jit(solution)/shard_map/ppermute | solution.py:449
  68.0 4.9 %shard_map.87.refs_0_ = bf16[624,1024]{1,0:T(8,128)(2,1)} custom-call(s32[17]{0:T(128)} %dynamic-slice_bitcast_fusion.scalars_ref, bf16[624,1024]{1,0:T(8,128)(2,1)} %get-tuple-element.9.x_ref, bf16[1024,8192]{1,0:T(8,128)(2,1)} %w_ref.17, bf16[624,1024]{1,0:T(8,128)(2,1)} %shard_map.86.refs_0_.refs_2_.refs_3_), custom_call_target="tpu_custom_call" | custom-call | flops 1308622848 | bytes 4653056 | tf_op jit(solution)/shard_map/pallas_call | solution.py:173
  74.4 5.2 %shard_map.88.refs_1_.rest_ref = f32[624,1024]{1,0:T(8,128)} custom-call(s32[17]{0:T(128)} %dynamic-slice_bitcast_fusion.scalars_ref, bf16[624,1024]{1,0:T(8,128)(2,1)} %get-tuple-element.9.x_ref, bf16[1024,8192]{1,0:T(8,128)(2,1)} %w_ref.17, bf16[624,1024]{1,0:T(8,128)(2,1)} %shard_map.87.refs_0_), custom_call_target="tpu_custom_call" | custom-call | flops 1308622848 | bytes 5931008 | tf_op jit(solution)/shard_map/pallas_call | solution.py:173
  79.5 7.5 %collective-permute-done.4.refs_0_ = bf16[624,1024]{1,0:T(8,128)(2,1)S(1)} collective-permute-done((bf16[624,1024]{1,0:T(8,128)(2,1)}, bf16[624,1024]{1,0:T(8,128)(2,1)S(1)}, u32[]{:S(2)}, u32[]{:S(2)}) %collective-permute-start.4) | collective-permute-done | bytes 1277984 | tf_op jit(solution)/shard_map/ppermute | solution.py:416
  88.1 5.1 %shard_map.89.sum_ref.refs_0_ = bf16[624,1024]{1,0:T(8,128)(2,1)} custom-call(s32[17]{0:T(128)} %dynamic-slice_bitcast_fusion.scalars_ref, bf16[624,1024]{1,0:T(8,128)(2,1)} %get-tuple-element.9.x_ref, bf16[1024,8192]{1,0:T(8,128)(2,1)} %w_ref.17, bf16[624,1024]{1,0:T(8,128)(2,1)} %copy-done, f32[624,1024]{1,0:T(8,128)} %shard_map.88.refs_1_.rest_ref), custom_call_target="tpu_custom_call" | custom-call | flops 1308622848 | bytes 5931008 | tf_op jit(solution)/shard_map/pallas_call | solution.py:173
  93.2 13.5 %collective-permute-done.5.got_ref = bf16[624,1024]{1,0:T(8,128)(2,1)S(1)} collective-permute-done((bf16[624,1024]{1,0:T(8,128)(2,1)}, bf16[624,1024]{1,0:T(8,128)(2,1)S(1)}, u32[]{:S(2)}, u32[]{:S(2)}) %collective-permute-start.5) | collective-permute-done | bytes 1277984 | tf_op jit(solution)/shard_map/ppermute | solution.py:449
  107.8 3.4 %shard_map.90.refs_0_ = bf16[624,1024]{1,0:T(8,128)(2,1)} custom-call(s32[17]{0:T(128)} %dynamic-slice_bitcast_fusion.scalars_ref, bf16[624,1024]{1,0:T(8,128)(2,1)} %shard_map.89.sum_ref.refs_0_, bf16[624,1024]{1,0:T(8,128)(2,1)} %copy-done.5, bf16[624,1024]{1,0:T(8,128)(2,1)} %shard_map.89.sum_ref.refs_0_), custom_call_target="tpu_custom_call" | custom-call | flops 1 | bytes 1 | tf_op jit(solution)/shard_map/pallas_call | solution.py:130
  111.9 4.9 %collective-permute-start.6 = (bf16[624,1024]{1,0:T(8,128)(2,1)}, bf16[624,1024]{1,0:T(8,128)(2,1)S(1)}, u32[]{:S(2)}, u32[]{:S(2)}) collective-permute-start(bf16[624,1024]{1,0:T(8,128)(2,1)} %shard_map.90.refs_0_), channel_id=1, source_target_pairs={{0,2},{1,3},{2,4},{3,5},{8,10},{9,11},{10,12},{11,13},{16,18},{17,... | collective-permute-start | bytes 3833864 | tf_op jit(solution)/shard_map/ppermute | solution.py:469
  116.8 4.9 %shard_map.91.refs_1_ = bf16[624,1024]{1,0:T(8,128)(2,1)} custom-call(s32[17]{0:T(128)} %dynamic-slice_bitcast_fusion.scalars_ref, bf16[624,1024]{1,0:T(8,128)(2,1)} %get-tuple-element.9.x_ref, bf16[1024,8192]{1,0:T(8,128)(2,1)} %w_ref.17, bf16[624,1024]{1,0:T(8,128)(2,1)} %shard_map.90.refs_0_), custom_call_target="tpu_custom_call" | custom-call | flops 1308622848 | bytes 4653056 | tf_op jit(solution)/shard_map/pallas_call | solution.py:173
  124.3 5.1 %shard_map.92.sum_ref.refs_4_ = bf16[624,1024]{1,0:T(8,128)(2,1)} custom-call(s32[17]{0:T(128)} %dynamic-slice_bitcast_fusion.scalars_ref, bf16[624,1024]{1,0:T(8,128)(2,1)} %get-tuple-element.9.x_ref, bf16[1024,8192]{1,0:T(8,128)(2,1)} %w_ref.17, bf16[624,1024]{1,0:T(8,128)(2,1)} %copy-done.2, bf16[624,1024]{1,0:T(8,128)(2,1)} %shard_map.91.refs_1_), custom_call_target="tpu_custom_call" | custom-call | flops 1308622848 | bytes 5931008 | tf_op jit(solution)/shard_map/pallas_call | solution.py:173
  129.4 15.1 %collective-permute-done.6.refs_0_ = bf16[624,1024]{1,0:T(8,128)(2,1)S(1)} collective-permute-done((bf16[624,1024]{1,0:T(8,128)(2,1)}, bf16[624,1024]{1,0:T(8,128)(2,1)S(1)}, u32[]{:S(2)}, u32[]{:S(2)}) %collective-permute-start.6) | collective-permute-done | bytes 1277984 | tf_op jit(solution)/shard_map/ppermute | solution.py:469
  145.5 5.0 %shard_map.93 = (bf16[624,1024]{1,0:T(8,128)(2,1)}, bf16[624,1024]{1,0:T(8,128)(2,1)}) custom-call(s32[17]{0:T(128)} %dynamic-slice_bitcast_fusion.scalars_ref, bf16[624,1024]{1,0:T(8,128)(2,1)} %shard_map.92.sum_ref.refs_4_, bf16[624,1024]{1,0:T(8,128)(2,1)} %copy-done.7, bf16[624,1024]{1,0:T(8,128)(2,1)} %copy-done.6, ...), custom_call_target="tpu_custom_call" | custom-call | flops 1 | bytes 1 | tf_op jit(solution)/shard_map/pallas_call | solution.py:130
  151.8 8.7 %collective-permute-start.10 = (bf16[624,1024]{1,0:T(8,128)(2,1)}, bf16[624,1024]{1,0:T(8,128)(2,1)}, u32[]{:S(2)}, u32[]{:S(2)}) collective-permute-start(bf16[624,1024]{1,0:T(8,128)(2,1)} %get-tuple-element.11.refs_0_), channel_id=1, source_target_pairs={{0,2},{1,3},{2,4},{3,5},{4,6},{5,7},{8,10},{9,11},{10,12},{11,13},... | collective-permute-start | bytes 3833864 | tf_op jit(solution)/shard_map/ppermute | solution.py:469
  163.5 2.2 %reduce_sum.19.shrunk_ref = bf16[384,128]{1,0:T(8,128)(2,1)} reduce(f32[8,384,128]{2,1,0:T(8,128)} %bitcast.10, f32[]{:T(128)} %constant.34.clone.1), dimensions={0}, to_apply=%region_1.2 | reduce | flops 344064 | bytes 1671172 | tf_op jit(solution)/shard_map/reduce_sum | solution.py:437
  165.6 13.6 %shard_map.94.base_ref = f32[768,1024]{1,0:T(8,128)} custom-call(s32[768,128]{1,0:T(8,128)} %broadcast_in_dim.2.slot_ref, bf16[384,128]{1,0:T(8,128)(2,1)} %reduce_sum.19.shrunk_ref, bf16[2048,1024]{1,0:T(8,128)(2,1)} %bitcast.9, bf16[2048,1024]{1,0:T(8,128)(2,1)} %collective-permute-done.1.refs_1_.other_ref, f32[624,1024]{1,0:T(8,128)} %shard_map.88.refs_1_.rest_ref, ...), custom_call_target="tpu_custom_call" | custom-call | flops 1 | bytes 1 | tf_op jit(solution)/shard_map/pallas_call | solution.py:316
  179.2 4.4 %collective-permute-done.11.refs_1_ = bf16[624,1024]{1,0:T(8,128)(2,1)S(1)} collective-permute-done((bf16[624,1024]{1,0:T(8,128)(2,1)}, bf16[624,1024]{1,0:T(8,128)(2,1)S(1)}, u32[]{:S(2)}, u32[]{:S(2)}) %collective-permute-start.11) | collective-permute-done | bytes 1277984 | tf_op jit(solution)/shard_map/ppermute | solution.py:469
  185.0 4.4 %shard_map.95 = bf16[768,1024]{1,0:T(8,128)(2,1)} custom-call(f32[768,1024]{1,0:T(8,128)} %shard_map.94.base_ref, bf16[144,1024]{1,0:T(8,128)(2,1)} %get-tuple-element.14.kept_ref, bf16[144,1024]{1,0:T(8,128)(2,1)} %copy-done.8, bf16[624,1024]{1,0:T(8,128)(2,1)} %copy-done.3, bf16[624,1024]{1,0:T(8,128)(2,1)} %collective-permute-done.10.refs_0_, ...), custom_call_target="tpu_custom_call" | custom-call | flops 1 | bytes 1 | tf_op jit(solution)/shard_map/pallas_call | solution.py:348
  (50 shorter events, 19.4 us)
Async XLA Ops:
  7.4 153.1 %reduce-scatter.2.cloned.1.call-start = ((), (), s32[]{:S(2)}) async-start(), calls=%async_computation.1 | async-start | bytes 2949120 | tf_op jit(solution)/shard_map/reduce_scatter | solution.py:430
  7.4 26.3 %collective-permute-start = (bf16[2048,1024]{1,0:T(8,128)(2,1)}, bf16[2048,1024]{1,0:T(8,128)(2,1)}, u32[]{:S(2)}, u32[]{:S(2)}) collective-permute-start(bf16[2048,1024]{1,0:T(8,128)(2,1)} %bitcast.6), channel_id=1, source_target_pairs={{0,8},{8,0},{1,9},{9,1},{2,10},{10,2},{3,11},{11,3},{4,12},{12,4},... | collective-permute-start | bytes 12582920 | tf_op jit(solution)/shard_map/ppermute | solution.py:405
  7.8 25.9 %collective-permute-start.1 = (bf16[2048,1024]{1,0:T(8,128)(2,1)}, bf16[2048,1024]{1,0:T(8,128)(2,1)}, u32[]{:S(2)}, u32[]{:S(2)}) collective-permute-start(bf16[2048,1024]{1,0:T(8,128)(2,1)} %bitcast.8), channel_id=1, source_target_pairs={{0,8},{8,0},{1,9},{9,1},{2,10},{10,2},{3,11},{11,3},{4,12},{12,4},... | collective-permute-start | bytes 12582920 | tf_op jit(solution)/shard_map/ppermute | solution.py:406
  20.3 143.2 %all-gather.3.cloned.1.call-start = ((), (), s32[]{:S(2)}) async-start(), calls=%async_computation.2 | async-start | bytes 1769472 | tf_op jit(solution)/shard_map/all_gather | solution.py:436
  25.5 32.1 %collective-permute-start.2 = (bf16[624,1024]{1,0:T(8,128)(2,1)}, bf16[624,1024]{1,0:T(8,128)(2,1)S(1)}, u32[]{:S(2)}, u32[]{:S(2)}) collective-permute-start(bf16[624,1024]{1,0:T(8,128)(2,1)} %get-tuple-element.10.refs_0_), channel_id=1, source_target_pairs={{0,1},{1,0},{2,3},{3,2},{4,5},{5,4},{6,7},{7,6},{8,9},{9,8},{10,11... | collective-permute-start | bytes 3833864 | tf_op jit(solution)/shard_map/ppermute | solution.py:425
  28.5 5.1 %copy-start.9 = (s32[768,1]{0,1:T(1,128)S(1)}, s32[768,1]{0,1:T(1,128)}, u32[]{:S(2)}) copy-start(s32[768,1]{0,1:T(1,128)} %param.13) | copy-start | bytes 9220
  28.5 5.1 %copy-start.10 = (s32[64]{0:T(128)S(1)}, s32[64]{0:T(128)}, u32[]{:S(2)}) copy-start(s32[64]{0:T(128)} %param.14) | copy-start | bytes 772
  33.5 53.5 %collective-permute-start.4 = (bf16[624,1024]{1,0:T(8,128)(2,1)}, bf16[624,1024]{1,0:T(8,128)(2,1)S(1)}, u32[]{:S(2)}, u32[]{:S(2)}) collective-permute-start(bf16[624,1024]{1,0:T(8,128)(2,1)} %shard_map.84.refs_0_), channel_id=1, source_target_pairs={{0,1},{1,0},{2,3},{3,2},{4,5},{5,4},{6,7},{7,6},{8,9},{9,8},{10,11... | collective-permute-start | bytes 3833864 | tf_op jit(solution)/shard_map/ppermute | solution.py:416
  57.6 1.1 copy-start.1
  63.8 43.0 %collective-permute-start.5 = (bf16[624,1024]{1,0:T(8,128)(2,1)}, bf16[624,1024]{1,0:T(8,128)(2,1)S(1)}, u32[]{:S(2)}, u32[]{:S(2)}) collective-permute-start(bf16[624,1024]{1,0:T(8,128)(2,1)} %shard_map.86.refs_0_.refs_2_.refs_3_), channel_id=1, source_target_pairs={{0,2},{1,3},{6,4},{7,5},{8,10},{9,11},{14,12},{15,13},{16,18},{17,... | collective-permute-start | bytes 3833864 | tf_op jit(solution)/shard_map/ppermute | solution.py:449
  72.8 50.4 %collective-permute-start.3 = (bf16[624,1024]{1,0:T(8,128)(2,1)}, bf16[624,1024]{1,0:T(8,128)(2,1)S(1)}, u32[]{:S(2)}, u32[]{:S(2)}) collective-permute-start(bf16[624,1024]{1,0:T(8,128)(2,1)} %shard_map.87.refs_0_), channel_id=1, source_target_pairs={{0,1},{1,0},{2,3},{3,2},{4,5},{5,4},{6,7},{7,6},{8,9},{9,8},{10,11... | collective-permute-start | bytes 3833864 | tf_op jit(solution)/shard_map/ppermute | solution.py:416
  87.1 1.1 copy-start
  106.7 1.1 copy-start.5
  111.2 18.2 %collective-permute-start.7 = (bf16[624,1024]{1,0:T(8,128)(2,1)}, bf16[624,1024]{1,0:T(8,128)(2,1)S(1)}, u32[]{:S(2)}, u32[]{:S(2)}) collective-permute-start(bf16[624,1024]{1,0:T(8,128)(2,1)} %shard_map.90.refs_0_), channel_id=1, source_target_pairs={{4,2},{5,3},{6,4},{7,5},{12,10},{13,11},{14,12},{15,13},{20,18},{2... | collective-permute-start | bytes 3833864 | tf_op jit(solution)/shard_map/ppermute | solution.py:469
  111.9 32.6 %collective-permute-start.6 = (bf16[624,1024]{1,0:T(8,128)(2,1)}, bf16[624,1024]{1,0:T(8,128)(2,1)S(1)}, u32[]{:S(2)}, u32[]{:S(2)}) collective-permute-start(bf16[624,1024]{1,0:T(8,128)(2,1)} %shard_map.90.refs_0_), channel_id=1, source_target_pairs={{0,2},{1,3},{2,4},{3,5},{8,10},{9,11},{10,12},{11,13},{16,18},{17,... | collective-permute-start | bytes 3833864 | tf_op jit(solution)/shard_map/ppermute | solution.py:469
  121.7 57.5 %collective-permute-start.9 = (bf16[624,1024]{1,0:T(8,128)(2,1)}, bf16[624,1024]{1,0:T(8,128)(2,1)S(1)}, u32[]{:S(2)}, u32[]{:S(2)}) collective-permute-start(bf16[624,1024]{1,0:T(8,128)(2,1)} %shard_map.91.refs_1_), channel_id=1, source_target_pairs={{0,1},{1,0},{2,3},{3,2},{4,5},{5,4},{6,7},{7,6},{8,9},{9,8},{10,11... | collective-permute-start | bytes 3833864 | tf_op jit(solution)/shard_map/ppermute | solution.py:416
  129.4 15.1 %copy-start.6 = (bf16[624,1024]{1,0:T(8,128)(2,1)}, bf16[624,1024]{1,0:T(8,128)(2,1)S(1)}, u32[]{:S(2)}) copy-start(bf16[624,1024]{1,0:T(8,128)(2,1)S(1)} %collective-permute-done.7.refs_1_) | copy-start | bytes 3833860
  144.5 1.0 copy-start.7
  150.5 33.2 %collective-permute-start.11 = (bf16[624,1024]{1,0:T(8,128)(2,1)}, bf16[624,1024]{1,0:T(8,128)(2,1)S(1)}, u32[]{:S(2)}, u32[]{:S(2)}) collective-permute-start(bf16[624,1024]{1,0:T(8,128)(2,1)} %get-tuple-element.12), channel_id=1, source_target_pairs={{2,0},{3,1},{4,2},{5,3},{6,4},{7,5},{10,8},{11,9},{12,10},{13,11},... | collective-permute-start | bytes 3833864 | tf_op jit(solution)/shard_map/ppermute | solution.py:469
  151.8 33.2 %collective-permute-start.10 = (bf16[624,1024]{1,0:T(8,128)(2,1)}, bf16[624,1024]{1,0:T(8,128)(2,1)}, u32[]{:S(2)}, u32[]{:S(2)}) collective-permute-start(bf16[624,1024]{1,0:T(8,128)(2,1)} %get-tuple-element.11.refs_0_), channel_id=1, source_target_pairs={{0,2},{1,3},{2,4},{3,5},{4,6},{5,7},{8,10},{9,11},{10,12},{11,13},... | collective-permute-start | bytes 3833864 | tf_op jit(solution)/shard_map/ppermute | solution.py:469
  162.3 16.9 %collective-permute-start.8 = (bf16[144,1024]{1,0:T(8,128)(2,1)S(1)}, bf16[144,1024]{1,0:T(8,128)(2,1)S(1)}, u32[]{:S(2)}, u32[]{:S(2)}) collective-permute-start(bf16[144,1024]{1,0:T(8,128)(2,1)S(1)} %get-tuple-element.13), channel_id=1, source_target_pairs={{0,1},{1,0},{2,3},{3,2},{4,5},{5,4},{6,7},{7,6},{8,9},{9,8},{10,11... | collective-permute-start | bytes 884744 | tf_op jit(solution)/shard_map/ppermute | solution.py:435
  179.2 5.8 %copy-start.8 = (bf16[144,1024]{1,0:T(8,128)(2,1)}, bf16[144,1024]{1,0:T(8,128)(2,1)S(1)}, u32[]{:S(2)}) copy-start(bf16[144,1024]{1,0:T(8,128)(2,1)S(1)} %collective-permute-done.8.part_ref) | copy-start | bytes 884740
  179.2 5.7 %copy-start.3 = (bf16[624,1024]{1,0:T(8,128)(2,1)}, bf16[624,1024]{1,0:T(8,128)(2,1)S(1)}, u32[]{:S(2)}) copy-start(bf16[624,1024]{1,0:T(8,128)(2,1)S(1)} %collective-permute-done.9.y_ref) | copy-start | bytes 3833860
  183.7 1.3 copy-start.4
  (1 other events, 1.0 us)
Sparse Core Ops, SparseCore 0:
  20.4 50.9 reduce-scatter.1
Sparse Core Ops, SparseCore 1:
  68.0 58.0 all-gather.2

commit v2 on v1

--- a/solution.py
+++ b/solution.py
@@ -10,12 +10,11 @@
 
 F32 = jnp.float32
 BF16 = jnp.bfloat16
-VMEM_BYTES = 56 * 2**20
 SMALL = pl.CostEstimate(flops=1, bytes_accessed=1, transcendentals=0)
 
 
-def params():
-    return pltpu.CompilerParams(vmem_limit_bytes=VMEM_BYTES)
+def params(large=False):
+    return pltpu.CompilerParams(vmem_limit_bytes=(56 if large else 32) * 2**20)
 
 
 def line_plan(places):
@@ -59,27 +58,23 @@
     return result
 
 
-def opening_body(scalars_ref, hidden_ref, scale_ref, w_ref, *refs):
-    rest_ref, away_ref = refs[-2:]
-    head = hidden_ref.shape[0] - rest_ref.shape[0]
-
+def opening_body(scalars_ref, hidden_ref, scale_ref, w_ref, x_ref, away_ref):
     @pl.when(pl.program_id(0) == 0)
     def _():
-        rest_ref[...] = (hidden_ref[head:].astype(F32) / scale_ref[...]).astype(BF16)
-
-    away_ref[...] = jnp.dot(rest_ref[...], w_ref[...], preferred_element_type=F32).astype(BF16)
-
-
-def opening(hidden, scale, weight, scalars, column, span, first, after=()):
+        x_ref[...] = (hidden_ref[...].astype(F32) / scale_ref[...]).astype(BF16)
+
+    away_ref[...] = jnp.dot(x_ref[...], w_ref[...], preferred_element_type=F32).astype(BF16)
+
+
+def opening(hidden, scale, weight, scalars, column, span):
     rows, depth = hidden.shape
-    rest = rows - first
     tile = min(512, span)
     whole = lambda j, s: (0, 0)
     return pl.pallas_call(
         opening_body,
         out_shape=[
-            jax.ShapeDtypeStruct((rest, depth), BF16),
-            jax.ShapeDtypeStruct((rest, span), BF16),
+            jax.ShapeDtypeStruct((rows, depth), BF16),
+            jax.ShapeDtypeStruct((rows, span), BF16),
         ],
         grid_spec=pltpu.PrefetchScalarGridSpec(
             num_scalar_prefetch=1,
@@ -88,24 +83,45 @@
                 pl.BlockSpec((rows, depth), whole),
                 pl.BlockSpec((1, depth), whole),
                 pl.BlockSpec((depth, tile), lambda j, s: (0, s[column] * (span // tile) + j)),
-            ]
-            + [pl.BlockSpec(memory_space=pl.ANY)] * len(after),
+            ],
             out_specs=[
-                pl.BlockSpec((rest, depth), whole),
-                pl.BlockSpec((rest, tile), lambda j, s: (0, j)),
+                pl.BlockSpec((rows, depth), whole),
+                pl.BlockSpec((rows, tile), lambda j, s: (0, j)),
             ],
         ),
+        compiler_params=params(True),
+        cost_estimate=SMALL,
+    )(scalars, hidden, scale.reshape(1, depth), weight)
+
+
+def merge_body(total_ref, got_ref, *refs):
+    total_out, sent_out = refs[-2:]
+    total = total_ref[...] + got_ref[...].astype(F32)
+    total_out[...] = total
+    sent_out[...] = total.astype(BF16)
+
+
+def merge(total, got, after=()):
+    block = pl.BlockSpec(total.shape, lambda: (0, 0))
+    return pl.pallas_call(
+        merge_body,
+        out_shape=[jax.ShapeDtypeStruct(total.shape, F32), jax.ShapeDtypeStruct(total.shape, BF16)],
+        in_specs=[block, block] + [pl.BlockSpec(memory_space=pl.ANY)] * len(after),
+        out_specs=[block, block],
         compiler_params=params(),
         cost_estimate=SMALL,
-    )(scalars, hidden, scale.reshape(1, depth), weight, *after)
-
-
-def product_body(added, scalars_ref, x_ref, w_ref, *refs):
+    )(total, got, *after)
+
+
+def product_body(added, more, scalars_ref, x_ref, w_ref, *refs):
     out_ref = refs[-1]
     total = jnp.dot(x_ref[...], w_ref[...], preferred_element_type=F32)
     for ref in refs[:added]:
         total = total + ref[...].astype(F32)
-    out_ref[...] = total.astype(out_ref.dtype)
+    rows = x_ref.shape[0]
+    out_ref[:rows] = total.astype(out_ref.dtype)
+    if more:
+        out_ref[rows:] = refs[added][...]
 
 
 def sums_body(column, flagged, scalars_ref, sum_ref, *refs):
@@ -162,17 +178,18 @@
     )(total, got, *after)
 
 
-def product(x, weight, scalars, column, span, adds=(), after=(), dtype=BF16, rows=None, block=0, tile=512):
+def product(x, weight, scalars, column, span, adds=(), after=(), dtype=BF16, rows=None, block=0, tile=512, tail=None, more=None):
     depth = x.shape[1]
     rows = rows or x.shape[0]
     tile = min(tile, span)
     steps = span // tile
-    out_block = pl.BlockSpec((rows, tile), lambda j, s: (0, j))
-    size = jnp.dtype(dtype).itemsize
-    out_shape = jax.ShapeDtypeStruct((rows, span), dtype)
-    return pl.pallas_call(
-        functools.partial(product_body, len(adds)),
-        out_shape=out_shape,
+    more = 0 if tail is None else more or tail.shape[0]
+    out_block = pl.BlockSpec((rows + more, tile), lambda j, s: (0, j))
+    block_in = pl.BlockSpec((rows, tile), lambda j, s: (0, j))
+    tails = [] if tail is None else [tail]
+    return pl.pallas_call(
+        functools.partial(product_body, len(adds), more),
+        out_shape=jax.ShapeDtypeStruct((rows + more, span), dtype),
         grid_spec=pltpu.PrefetchScalarGridSpec(
             num_scalar_prefetch=1,
             grid=(steps,),
@@ -181,19 +198,16 @@
                 pl.BlockSpec((depth, tile), lambda j, s: (0, s[column] * steps + j)),
             ]
             + [
-                out_block if a.shape[0] == rows else pl.BlockSpec((rows, tile), lambda j, s: (block, j))
+                block_in if a.shape[0] == rows else pl.BlockSpec((rows, tile), lambda j, s: (block, j))
                 for a in adds
             ]
+            + [pl.BlockSpec((more, tile), lambda j, s: (0, j)) for _ in tails]
             + [pl.BlockSpec(memory_space=pl.ANY)] * len(after),
             out_specs=out_block,
         ),
-        compiler_params=params(),
-        cost_estimate=pl.CostEstimate(
-            flops=2 * rows * depth * span,
-            bytes_accessed=2 * rows * depth + 2 * depth * span + rows * span * (size + 2 * len(adds)),
-            transcendentals=0,
-        ),
-    )(scalars, x, weight, *adds, *after)
+        compiler_params=params(True),
+        cost_estimate=SMALL,
+    )(scalars, x, weight, *adds, *tails, *after)
 
 
 def holds(slot, first, rank):
@@ -303,9 +317,7 @@
     @pl.when(j == pl.num_programs(0) - 1)
     def _():
         delta = 0.5 * total[...].astype(BF16).astype(F32)
-        head = delta.shape[0] - rest_ref.shape[0]
-        out_ref[:head] = delta[:head]
-        out_ref[head:] = rest_ref[...] + delta[head:]
+        out_ref[...] = rest_ref[...] + delta
 
 
 def expand_rows(shrunk, own, other, slot, rank, rest, after=()):
@@ -328,23 +340,20 @@
     )(slot, shrunk, own, other, rest, *after)
 
 
-def finish_body(blocks, base_ref, kept_ref, part_ref, y_ref, *refs):
+def finish_body(blocks, base_ref, y_ref, *refs):
     ends, out_ref = refs[: 2 * blocks], refs[-1]
     size = ends[0].shape[0]
-    head = base_ref.shape[0] - blocks * size
-    total = base_ref[:head] + kept_ref[...].astype(F32) + part_ref[...].astype(F32)
-    out_ref[:head] = total.astype(out_ref.dtype)
     for b in range(blocks):
-        at = slice(head + b * size, head + (b + 1) * size)
-        total = base_ref[at] + y_ref[b * size : (b + 1) * size].astype(F32)
+        at = slice(b * size, (b + 1) * size)
+        total = base_ref[at] + y_ref[at].astype(F32)
         total = total + ends[2 * b][...].astype(F32) + ends[2 * b + 1][...].astype(F32)
         out_ref[at] = total.astype(out_ref.dtype)
 
 
-def finish(base, kept, part, y_part, ends):
+def finish(base, y_part, ends):
     rows, width = base.shape
     tile = min(width, 512)
-    operands = [base, kept, part, y_part] + [end for pair in ends for end in pair]
+    operands = [base, y_part] + [end for pair in ends for end in pair]
     return pl.pallas_call(
         functools.partial(finish_body, len(ends)),
         out_shape=jax.ShapeDtypeStruct((rows, width), BF16),
@@ -377,8 +386,8 @@
     o = lax.axis_index("owner")
     swap_y = [(i, i ^ 1) for i in range(tensors)]
     swap_owner = [(0, 1), (1, 0)]
-    first = rows // 256 * 48
-    lines = [list(range(i, tensors, 2)) for i in range(2)]
+    blocks = 2
+    part = rows // blocks
     order, up, down = line_plan(places)
     final = places - 1
     table = [
@@ -392,13 +401,11 @@
                 down.get((final, i // 2)) == final - 1,
             )
         ]
-        + [0]
         for i in range(tensors)
     ]
     scalars = lax.dynamic_index_in_dim(jnp.asarray(np.array(table, np.int32)), t, keepdims=False)
     away_at = list(range(places))
     here_at = [places + 3 * k for k in range(places)]
-    zero_at = 4 * places
 
     shrink = shrink_matrix_bank.reshape(resident * rank, depth)
     expand = expand_matrix_bank.reshape(resident * rank, width)
@@ -411,72 +418,86 @@
     slot = jnp.where(slot < o * resident, slot + adapters, slot) - o * resident
     slot = jnp.broadcast_to(slot, (rows, 2 * rank))
 
+    def there(k, last, tail=None):
+        more = None
+        if k == 1:
+            tail, more = x, rows * rank // width + 16
+        return product(x, weight, scalars, away_at[k], width, after=(last,), tail=tail, more=more)
+
+    tails = {}
+
     def send_along_y(k, last):
-        sent = product(x_rest, weight, scalars, away_at[k], width, after=(last,))
+        sent = there(k, last, tails.get(k))
         y_got.append(lax.ppermute(sent, "tensor", swap_y))
         return sent
 
-    x_first = (hidden[:first].astype(F32) / channel_smooth_scale).astype(BF16)
-    z_all = product(x_first, weight, scalars, zero_at, 2 * width * places, tile=2048)
-
-    x_rest, away = opening(
-        hidden, channel_smooth_scale, weight, scalars, away_at[0], width, first, after=(z_all,)
-    )
+    x, away = opening(hidden, channel_smooth_scale, weight, scalars, away_at[0], width)
     y_got = [lax.ppermute(away, "tensor", swap_y)]
-    last = send_along_y(1, away)
-    last = part_sum = shrink_rows(
-        hidden, shrink, shrink_other, slot, rank, after=(last, expand_other)
-    )
-    z_sum = lax.psum_scatter(
-        z_all, "tensor", scatter_dimension=1, axis_index_groups=lines, tiled=True
-    )
-    z_sent = jnp.where(y == 0, z_sum[:, width:], z_sum[:, :width])
-    z_kept = jnp.where(y == 0, z_sum[:, :width], z_sum[:, width:])
-    z_part = lax.ppermute(z_sent, "tensor", swap_y)
-    every = lax.all_gather(part_sum, "tensor", axis=0)
-    shrunk = jnp.sum(every, axis=0).astype(BF16)
+
+    last = total = shrink_rows(hidden, shrink, shrink_other, slot, rank, after=(away, expand_other))
+    sent = total.astype(BF16)
+    for i in range(1, tensors.bit_length() - 1):
+        pairs = [(j, j ^ 2**i) for j in range(tensors)]
+        got = lax.ppermute(sent, "tensor", pairs)
+        if i == 1:
+            last = send_along_y(1, last)
+        if i == 2:
+            last = own = product(x, weight, scalars, here_at[final], width, after=(last,), dtype=F32)
+        total, sent = merge(total, got, after=(last,))
+        last = total
+    tails[2] = sent.reshape(-1, width)
 
     values = []
-    arrived = ()
+    arrived = [()] * blocks
     for s in range(1, places):
         k = s - 1
         ups = [(a * 2 + i, a * 2 + 2 + i) for a in range(places - 1) for i in range(2) if a <= s - 1]
         downs = [(a * 2 + i, a * 2 - 2 + i) for a in range(1, places) for i in range(2) if a >= places - s]
-        last = whole = product(
-            x_rest, weight, scalars, here_at[k], width, (y_got[k],), after=(last,)
-        )
         if s == 1:
-            arrived = (lax.ppermute(last, "tensor", ups + downs),)
-        else:
+            last = send_along_y(s + 1, last)
+        parts = []
+        if s > 1:
+            last = whole = product(
+                x, weight, scalars, here_at[k], width, (y_got[k],), after=(last,), dtype=F32
+            )
+        for b in range(blocks):
+            if s == 1:
+                last = product(
+                    x, weight, scalars, here_at[k], width, (y_got[k],), after=(last,), rows=part, block=b
+                )
+                arrived[b] = (lax.ppermute(last, "tensor", ups + downs),)
+                parts.append(last)
+                continue
+            cut = slice(b * part, (b + 1) * part)
             if 2 * s <= places:
-                if len(arrived) == 1:
-                    last = whole = sums(scalars, 0, whole, 0, arrived, after=(last,))[0]
+                if len(arrived[b]) == 1:
+                    last = sums(scalars, 0, whole, b, arrived[b], after=(last,))[0]
                 else:
-                    whole = whole.astype(F32) + arrived[0].astype(F32) + arrived[1].astype(F32)
-                    whole = last = whole.astype(BF16)
-                outs = whole, whole
+                    last = whole[cut].astype(F32) + arrived[b][0].astype(F32) + arrived[b][1].astype(F32)
+                    last = last.astype(BF16)
+                outs = last, last
+                parts.append(last)
             else:
-                got = arrived if len(arrived) == 2 else arrived * 2
+                got = arrived[b] if len(arrived[b]) == 2 else arrived[b] * 2
+                earlier = [value[b] for value in values]
                 if s < final:
+                    parts.append(whole[cut])
                     outs = [
-                        (pick(z, table, s, places, values + [whole]).astype(F32) + one.astype(F32)).astype(BF16)
+                        (pick(z, table, s, places, earlier + parts[-1:]).astype(F32) + one.astype(F32)).astype(BF16)
                         for table, one in zip((up, down), got)
                     ]
                 else:
-                    others = [pick(z, table, s, places, values) for table in (up, down)]
-                    outs = sums(scalars, here_at[k], whole, 0, got, others, after=(last,))
+                    others = [pick(z, table, s, places, earlier) for table in (up, down)]
+                    outs = sums(scalars, here_at[k], whole, b, got, others, after=(last,))
                 last = outs[0]
-            arrived = lax.ppermute(outs[0], "tensor", ups), lax.ppermute(outs[1], "tensor", downs)
-        values.append(whole)
-        if s + 1 < places:
+            arrived[b] = lax.ppermute(outs[0], "tensor", ups), lax.ppermute(outs[1], "tensor", downs)
+        values.append(parts)
+        if 1 < s < final:
             last = send_along_y(s + 1, last)
-        if s == 1:
-            last = own = product(
-                x_rest, weight, scalars, here_at[final], width, after=(last,), dtype=F32
-            )
-
+
+    shrunk = (total + y_got[2][rows:].reshape(total.shape).astype(F32)).astype(BF16)
     base = expand_rows(shrunk, expand, expand_other, slot, rank, own, after=(last,))
-    return finish(base, z_kept, z_part, y_got[-1], [arrived])
+    return finish(base, y_got[-1], arrived)
 
 
 def solution(mesh):

time: 198 us -> 176 us (0.89)
  waiting for transfers between devices: 52.8 us -> 35.2 us
  between operations: 15 us -> 0.36 us
  starting transfers between devices: 27.6 us -> 39.3 us
  local copies, waits for them, and re-layouts: 7.49 us -> 18.6 us
  Pallas kernels: 88.1 us -> 78.4 us
  other arithmetic: 5.83 us -> 2.75 us
    ppermute x2 -> x4, waiting for transfers between devices: 16.4 us -> 4.75 us  [shards(): lax.ppermute(outs[0], 'tensor', ups)]
    ppermute x3, waiting for transfers between devices: 7.54 us -> 19 us  [send_along_y(): y_got.append(lax.ppermute(sent, 'tensor', swap_y))]
    ppermute x1, waiting for transfers between devices: 10.9 us -> 0.01 us  [shards(): y_got = [lax.ppermute(away, 'tensor', swap_y)]]
    ppermute x2 -> x4, waiting for transfers between devices: 13.5 us -> 3.57 us  [the longest x2 3.57 us: shards(): arrived[b] = (lax.ppermute(last, 'tensor', ups + downs),)]
    unnamed x22 -> x42, local copies, waits for them, and re-layouts: 5.34 us -> 14.9 us
    ppermute x2 -> x4, starting transfers between devices: 13.6 us -> 18.3 us  [shards(): lax.ppermute(outs[0], 'tensor', ups)]
    ppermute x2 -> x4, starting transfers between devices: 5.34 us -> 9.58 us  [the longest x2 5.6 us: shards(): got = lax.ppermute(sent, 'tensor', pairs)]
    pallas_call x1, Pallas kernels: 13.6 us -> 10.3 us  [expand_rows(): pl.pallas_call(functools.partial(expand_body, rank), out_shape=jax.ShapeD...]
  transfers between devices with their start and end apart: 14 -> 18, of which waited for: 6 -> 6; matrix products, arithmetic and copies ran while one was open for 4% -> 4% of each run, Pallas kernels for 43% -> 43%
where the time goes in v2:
time: 176 us; the launch traced here: 175 us
  Pallas kernels  78.4 us (45%)
  starting transfers between devices  39.3 us (22%)
  waiting for transfers between devices  35.2 us (20%)
  local copies, waits for them, and re-layouts  18.6 us (11%)
  other arithmetic  2.75 us (2%)
    pallas_call x8, Pallas kernels, product(): pl.pallas_call(functools.partial(product_body, len(adds), more), out_shap...  42.2 us
    ppermute x3, waiting for transfers between devices, send_along_y(): y_got.append(lax.ppermute(sent, 'tensor', swap_y))  19 us
    ppermute x4, starting transfers between devices, shards(): lax.ppermute(outs[0], 'tensor', ups)  18.3 us
    unnamed x42, local copies, waits for them, and re-layouts  14.9 us
    pallas_call x1, Pallas kernels, expand_rows(): pl.pallas_call(functools.partial(expand_body, rank), out_shape=jax.ShapeD...  10.3 us
    pallas_call x1, Pallas kernels, shrink_rows(): pl.pallas_call(functools.partial(shrink_body, rank), out_shape=jax.ShapeD...  10.1 us
    pallas_call x4, Pallas kernels, sums(): pl.pallas_call(functools.partial(sums_body, column, count) if count else...  6.31 us
    pallas_call x1, Pallas kernels, opening(): pl.pallas_call(opening_body, out_shape=[jax.ShapeDtypeStruct((rows, depth...  5.76 us
  transfers between devices with their start and end apart: 18, of which 6 were waited for; matrix products, arithmetic and copies ran while one was open for 4% of the time, Pallas kernels for 43%

profile of v2, /device:TPU:0, one launch (start us, length us, event | category | flops | bytes accessed | tf_op | source)
XLA Modules:
  0.0 174.7 jit_solution(5943627573628724392)
XLA Ops:
  1.8 5.8 %shard_map.82 = (bf16[768,1024]{1,0:T(8,128)(2,1)}, bf16[768,1024]{1,0:T(8,128)(2,1)}) custom-call(s32[16]{0:T(128)} %dynamic-slice_bitcast_fusion.scalars_ref, bf16[768,1024]{1,0:T(8,128)(2,1)} %x_ref.1, f32[1,1024]{1,0:T(1,128)} %bitcast.9, bf16[1024,8192]{1,0:T(8,128)(2,1)} %w_ref.17), custom_call_target="tpu_custom_call" | custom-call | flops 1 | bytes 1 | tf_op jit(solution)/shard_map/pallas_call | solution.py:73
  7.5 3.0 %collective-permute-start.6 = (bf16[768,1024]{1,0:T(8,128)(2,1)}, bf16[768,1024]{1,0:T(8,128)(2,1)S(1)}, u32[]{:S(2)}, u32[]{:S(2)}) collective-permute-start(bf16[768,1024]{1,0:T(8,128)(2,1)} %get-tuple-element.15.refs_0_), channel_id=1, source_target_pairs={{0,1},{1,0},{2,3},{3,2},{4,5},{5,4},{6,7},{7,6},{8,9},{9,8},{10,11... | collective-permute-start | bytes 4718600 | tf_op jit(solution)/shard_map/ppermute | solution.py:435
  10.7 2.9 %collective-permute-done.1.refs_1_.other_ref = bf16[2048,1024]{1,0:T(8,128)(2,1)} collective-permute-done((bf16[2048,1024]{1,0:T(8,128)(2,1)}, bf16[2048,1024]{1,0:T(8,128)(2,1)}, u32[]{:S(2)}, u32[]{:S(2)}) %collective-permute-start.1) | collective-permute-done | bytes 4194336 | tf_op jit(solution)/shard_map/ppermute | solution.py:413
  17.4 10.1 %shard_map.83.refs_1_.total_ref = f32[384,128]{1,0:T(8,128)S(1)} custom-call(s32[768,128]{1,0:T(8,128)S(1)} %broadcast_in_dim.2.slot_ref, bf16[768,1024]{1,0:T(8,128)(2,1)S(1)} %copy-done.6, bf16[2048,1024]{1,0:T(8,128)(2,1)S(1)} %bitcast.6, bf16[2048,1024]{1,0:T(8,128)(2,1)} %collective-permute-done.other_ref, bf16[768,1024]{1,0:T(8,128)(2,1)S(1)} %copy-done.12, ...), custom_call_target="tpu_custom_call" | custom-call | flops 1 | bytes 1 | tf_op jit(solution)/shard_map/pallas_call | solution.py:273
  27.5 3.0 %collective-permute-start.2 = (bf16[384,128]{1,0:T(8,128)(2,1)S(1)}, bf16[384,128]{1,0:T(8,128)(2,1)S(1)}, u32[]{:S(2)}, u32[]{:S(2)}) collective-permute-start(bf16[384,128]{1,0:T(8,128)(2,1)S(1)} %convert_element_type.13), channel_id=1, source_target_pairs={{0,2},{1,3},{2,0},{3,1},{4,6},{5,7},{6,4},{7,5},{8,10},{9,11},{10,... | collective-permute-start | bytes 294920 | tf_op jit(solution)/shard_map/ppermute | solution.py:441
  30.5 5.4 %shard_map.84.refs_0_ = bf16[832,1024]{1,0:T(8,128)(2,1)} custom-call(s32[16]{0:T(128)} %dynamic-slice_bitcast_fusion.scalars_ref, bf16[768,1024]{1,0:T(8,128)(2,1)} %get-tuple-element.16.x_ref.refs_0_, bf16[1024,8192]{1,0:T(8,128)(2,1)} %w_ref.17, bf16[768,1024]{1,0:T(8,128)(2,1)} %get-tuple-element.16.x_ref.refs_0_, f32[384,128]{1,0:T(8,128)} %copy-done.9), custom_call_target="tpu_custom_call" | custom-call | flops 1 | bytes 1 | tf_op jit(solution)/shard_map/pallas_call | solution.py:190
  41.7 5.7 %shard_map.86.refs_0_.rest_ref = f32[768,1024]{1,0:T(8,128)} custom-call(s32[16]{0:T(128)} %dynamic-slice_bitcast_fusion.scalars_ref, bf16[768,1024]{1,0:T(8,128)(2,1)} %get-tuple-element.16.x_ref.refs_0_, bf16[1024,8192]{1,0:T(8,128)(2,1)} %w_ref.17, f32[384,128]{1,0:T(8,128)} %copy-done.14), custom_call_target="tpu_custom_call" | custom-call | flops 1 | bytes 1 | tf_op jit(solution)/shard_map/pallas_call | solution.py:190
  50.7 5.4 %shard_map.88.refs_1_ = bf16[816,1024]{1,0:T(8,128)(2,1)} custom-call(s32[16]{0:T(128)} %dynamic-slice_bitcast_fusion.scalars_ref, bf16[768,1024]{1,0:T(8,128)(2,1)} %get-tuple-element.16.x_ref.refs_0_, bf16[1024,8192]{1,0:T(8,128)(2,1)} %w_ref.17, bf16[48,1024]{1,0:T(8,128)(2,1)} %reshape.29.refs_0_, f32[384,128]{1,0:T(8,128)} %copy-done.13), custom_call_target="tpu_custom_call" | custom-call | flops 1 | bytes 1 | tf_op jit(solution)/shard_map/pallas_call | solution.py:190
  57.8 4.2 %shard_map.89.refs_1_.refs_2_.refs_3_ = bf16[384,1024]{1,0:T(8,128)(2,1)} custom-call(s32[16]{0:T(128)} %dynamic-slice_bitcast_fusion.scalars_ref, bf16[768,1024]{1,0:T(8,128)(2,1)} %get-tuple-element.16.x_ref.refs_0_, bf16[1024,8192]{1,0:T(8,128)(2,1)} %w_ref.17, bf16[768,1024]{1,0:T(8,128)(2,1)} %copy-done.18, bf16[816,1024]{1,0:T(8,128)(2,1)} %shard_map.88.refs_1_), custom_call_target="tpu_custom_call" | custom-call | flops 1 | bytes 1 | tf_op jit(solution)/shard_map/pallas_call | solution.py:190
  64.6 4.3 %shard_map.90.refs_1_.refs_2_.refs_3_ = bf16[384,1024]{1,0:T(8,128)(2,1)} custom-call(s32[16]{0:T(128)} %dynamic-slice_bitcast_fusion.scalars_ref, bf16[768,1024]{1,0:T(8,128)(2,1)} %get-tuple-element.16.x_ref.refs_0_, bf16[1024,8192]{1,0:T(8,128)(2,1)} %w_ref.17, bf16[768,1024]{1,0:T(8,128)(2,1)} %copy-done.18, ...), custom_call_target="tpu_custom_call" | custom-call | flops 1 | bytes 1 | tf_op jit(solution)/shard_map/pallas_call | solution.py:190
  70.3 12.3 %collective-permute-done.5.refs_0_ = bf16[832,1024]{1,0:T(8,128)(2,1)} collective-permute-done((bf16[832,1024]{1,0:T(8,128)(2,1)}, bf16[832,1024]{1,0:T(8,128)(2,1)}, u32[]{:S(2)}, u32[]{:S(2)}) %collective-permute-start.5) | collective-permute-done | bytes 1703968 | tf_op jit(solution)/shard_map/ppermute | solution.py:431
  82.6 5.8 %shard_map.91.sum_ref.refs_0_ = f32[768,1024]{1,0:T(8,128)} custom-call(s32[16]{0:T(128)} %dynamic-slice_bitcast_fusion.scalars_ref, bf16[768,1024]{1,0:T(8,128)(2,1)} %get-tuple-element.16.x_ref.refs_0_, bf16[1024,8192]{1,0:T(8,128)(2,1)} %w_ref.17, bf16[832,1024]{1,0:T(8,128)(2,1)} %collective-permute-done.5.refs_0_, ...), custom_call_target="tpu_custom_call" | custom-call | flops 1 | bytes 1 | tf_op jit(solution)/shard_map/pallas_call | solution.py:190
  91.3 4.1 %collective-permute-start.11 = (bf16[384,1024]{1,0:T(8,128)(2,1)S(1)}, bf16[384,1024]{1,0:T(8,128)(2,1)S(1)}, u32[]{:S(2)}, u32[]{:S(2)}) collective-permute-start(bf16[384,1024]{1,0:T(8,128)(2,1)S(1)} %shard_map.92.refs_0_), channel_id=1, source_target_pairs={{0,2},{1,3},{2,4},{3,5},{8,10},{9,11},{10,12},{11,13},{16,18},{17,... | collective-permute-start | bytes 2359304 | tf_op jit(solution)/shard_map/ppermute | solution.py:493
  96.1 3.6 %collective-permute-done.7.got_ref = bf16[384,1024]{1,0:T(8,128)(2,1)S(1)} collective-permute-done((bf16[384,1024]{1,0:T(8,128)(2,1)}, bf16[384,1024]{1,0:T(8,128)(2,1)S(1)}, u32[]{:S(2)}, u32[]{:S(2)}) %collective-permute-start.7) | collective-permute-done | bytes 786464 | tf_op jit(solution)/shard_map/ppermute | solution.py:468
  100.6 4.3 %collective-permute-start.9 = (bf16[384,1024]{1,0:T(8,128)(2,1)S(1)}, bf16[384,1024]{1,0:T(8,128)(2,1)S(1)}, u32[]{:S(2)}, u32[]{:S(2)}) collective-permute-start(bf16[384,1024]{1,0:T(8,128)(2,1)S(1)} %shard_map.93.refs_0_), channel_id=1, source_target_pairs={{0,2},{1,3},{2,4},{3,5},{8,10},{9,11},{10,12},{11,13},{16,18},{17,... | collective-permute-start | bytes 2359304 | tf_op jit(solution)/shard_map/ppermute | solution.py:493
  105.7 5.3 %shard_map.94.refs_1_ = bf16[768,1024]{1,0:T(8,128)(2,1)} custom-call(s32[16]{0:T(128)} %dynamic-slice_bitcast_fusion.scalars_ref, bf16[768,1024]{1,0:T(8,128)(2,1)} %get-tuple-element.16.x_ref.refs_0_, bf16[1024,8192]{1,0:T(8,128)(2,1)} %w_ref.17, bf16[384,1024]{1,0:T(8,128)(2,1)} %copy-done.11), custom_call_target="tpu_custom_call" | custom-call | flops 1 | bytes 1 | tf_op jit(solution)/shard_map/pallas_call | solution.py:190
  111.0 6.7 %collective-permute-done.4.refs_0_ = bf16[816,1024]{1,0:T(8,128)(2,1)} collective-permute-done((bf16[816,1024]{1,0:T(8,128)(2,1)}, bf16[816,1024]{1,0:T(8,128)(2,1)}, u32[]{:S(2)}, u32[]{:S(2)}) %collective-permute-start.4) | collective-permute-done | bytes 1671200 | tf_op jit(solution)/shard_map/ppermute | solution.py:431
  119.5 6.0 %shard_map.95.sum_ref.refs_4_ = f32[768,1024]{1,0:T(8,128)} custom-call(s32[16]{0:T(128)} %dynamic-slice_bitcast_fusion.scalars_ref, bf16[768,1024]{1,0:T(8,128)(2,1)} %get-tuple-element.16.x_ref.refs_0_, bf16[1024,8192]{1,0:T(8,128)(2,1)} %w_ref.17, bf16[816,1024]{1,0:T(8,128)(2,1)} %collective-permute-done.4.refs_0_, bf16[768,1024]{1,0:T(8,128)(2,1)} %shard_map.94.refs_1_), custom_call_target="tpu_custom_call" | custom-call | flops 1 | bytes 1 | tf_op jit(solution)/shard_map/pallas_call | solution.py:190
  129.6 4.3 %collective-permute-start.14 = (bf16[384,1024]{1,0:T(8,128)(2,1)}, bf16[384,1024]{1,0:T(8,128)(2,1)}, u32[]{:S(2)}, u32[]{:S(2)}) collective-permute-start(bf16[384,1024]{1,0:T(8,128)(2,1)} %get-tuple-element.21.refs_4_), channel_id=1, source_target_pairs={{0,2},{1,3},{2,4},{3,5},{4,6},{5,7},{8,10},{9,11},{10,12},{11,13},... | collective-permute-start | bytes 2359304 | tf_op jit(solution)/shard_map/ppermute | solution.py:493
  137.5 5.5 %collective-permute-start.16 = (bf16[384,1024]{1,0:T(8,128)(2,1)}, bf16[384,1024]{1,0:T(8,128)(2,1)}, u32[]{:S(2)}, u32[]{:S(2)}) collective-permute-start(bf16[384,1024]{1,0:T(8,128)(2,1)} %get-tuple-element.22.refs_0_), channel_id=1, source_target_pairs={{0,2},{1,3},{2,4},{3,5},{4,6},{5,7},{8,10},{9,11},{10,12},{11,13},... | collective-permute-start | bytes 2359304 | tf_op jit(solution)/shard_map/ppermute | solution.py:493
  150.9 10.3 %shard_map.98.base_ref = f32[768,1024]{1,0:T(8,128)S(1)} custom-call(s32[768,128]{1,0:T(8,128)S(1)} %broadcast_in_dim.2.slot_ref, bf16[384,128]{1,0:T(8,128)(2,1)S(1)} %add_convert_fusion.shrunk_ref, bf16[2048,1024]{1,0:T(8,128)(2,1)S(1)} %bitcast.8, bf16[2048,1024]{1,0:T(8,128)(2,1)} %collective-permute-done.1.refs_1_.other_ref, f32[768,1024]{1,0:T(8,128)S(1)} %copy-done.3, ...), custom_call_target="tpu_custom_call" | custom-call | flops 1 | bytes 1 | tf_op jit(solution)/shard_map/pallas_call | solution.py:328
  161.3 4.7 %collective-permute-done.16.refs_2_ = bf16[384,1024]{1,0:T(8,128)(2,1)} collective-permute-done((bf16[384,1024]{1,0:T(8,128)(2,1)}, bf16[384,1024]{1,0:T(8,128)(2,1)}, u32[]{:S(2)}, u32[]{:S(2)}) %collective-permute-start.16) | collective-permute-done | bytes 786464 | tf_op jit(solution)/shard_map/ppermute | solution.py:493
  166.0 5.0 %collective-permute-done.17.refs_3_ = bf16[384,1024]{1,0:T(8,128)(2,1)} collective-permute-done((bf16[384,1024]{1,0:T(8,128)(2,1)}, bf16[384,1024]{1,0:T(8,128)(2,1)}, u32[]{:S(2)}, u32[]{:S(2)}) %collective-permute-start.17) | collective-permute-done | bytes 786464 | tf_op jit(solution)/shard_map/ppermute | solution.py:493
  171.0 3.7 %shard_map.99 = bf16[768,1024]{1,0:T(8,128)(2,1)} custom-call(f32[768,1024]{1,0:T(8,128)S(1)} %shard_map.98.base_ref, bf16[768,1024]{1,0:T(8,128)(2,1)} %collective-permute-done.13.y_ref, bf16[384,1024]{1,0:T(8,128)(2,1)} %collective-permute-done.14.refs_0_, bf16[384,1024]{1,0:T(8,128)(2,1)} %collective-permute-done.15.refs_1_, ...), custom_call_target="tpu_custom_call" | custom-call | flops 1 | bytes 1 | tf_op jit(solution)/shard_map/pallas_call | solution.py:357
  (82 shorter events, 42.8 us)
Async XLA Ops:
  0.0 10.7 %collective-permute-start = (bf16[2048,1024]{1,0:T(8,128)(2,1)}, bf16[2048,1024]{1,0:T(8,128)(2,1)}, u32[]{:S(2)}, u32[]{:S(2)}) collective-permute-start(bf16[2048,1024]{1,0:T(8,128)(2,1)} %bitcast.5), channel_id=1, source_target_pairs={{0,8},{8,0},{1,9},{9,1},{2,10},{10,2},{3,11},{11,3},{4,12},{12,4},... | collective-permute-start | bytes 12582920 | tf_op jit(solution)/shard_map/ppermute | solution.py:412
  0.5 13.1 %collective-permute-start.1 = (bf16[2048,1024]{1,0:T(8,128)(2,1)}, bf16[2048,1024]{1,0:T(8,128)(2,1)}, u32[]{:S(2)}, u32[]{:S(2)}) collective-permute-start(bf16[2048,1024]{1,0:T(8,128)(2,1)} %bitcast.7), channel_id=1, source_target_pairs={{0,8},{8,0},{1,9},{9,1},{2,10},{10,2},{3,11},{11,3},{4,12},{12,4},... | collective-permute-start | bytes 12582920 | tf_op jit(solution)/shard_map/ppermute | solution.py:413
  1.8 12.0 %copy-start.6 = (bf16[768,1024]{1,0:T(8,128)(2,1)S(1)}, bf16[768,1024]{1,0:T(8,128)(2,1)}, u32[]{:S(2)}) copy-start(bf16[768,1024]{1,0:T(8,128)(2,1)} %x_ref.1) | copy-start | bytes 4718596
  7.5 49.1 %collective-permute-start.6 = (bf16[768,1024]{1,0:T(8,128)(2,1)}, bf16[768,1024]{1,0:T(8,128)(2,1)S(1)}, u32[]{:S(2)}, u32[]{:S(2)}) collective-permute-start(bf16[768,1024]{1,0:T(8,128)(2,1)} %get-tuple-element.15.refs_0_), channel_id=1, source_target_pairs={{0,1},{1,0},{2,3},{3,2},{4,5},{5,4},{6,7},{7,6},{8,9},{9,8},{10,11... | collective-permute-start | bytes 4718600 | tf_op jit(solution)/shard_map/ppermute | solution.py:435
  27.5 8.4 %collective-permute-start.2 = (bf16[384,128]{1,0:T(8,128)(2,1)S(1)}, bf16[384,128]{1,0:T(8,128)(2,1)S(1)}, u32[]{:S(2)}, u32[]{:S(2)}) collective-permute-start(bf16[384,128]{1,0:T(8,128)(2,1)S(1)} %convert_element_type.13), channel_id=1, source_target_pairs={{0,2},{1,3},{2,0},{3,1},{4,6},{5,7},{6,4},{7,5},{8,10},{9,11},{10,... | collective-permute-start | bytes 294920 | tf_op jit(solution)/shard_map/ppermute | solution.py:441
  37.6 9.9 %collective-permute-start.3 = (bf16[384,128]{1,0:T(8,128)(2,1)S(1)}, bf16[384,128]{1,0:T(8,128)(2,1)S(1)}, u32[]{:S(2)}, u32[]{:S(2)}) collective-permute-start(bf16[384,128]{1,0:T(8,128)(2,1)S(1)} %get-tuple-element.18), channel_id=1, source_target_pairs={{0,4},{1,5},{2,6},{3,7},{4,0},{5,1},{6,2},{7,3},{8,12},{9,13},{10,... | collective-permute-start | bytes 294920 | tf_op jit(solution)/shard_map/ppermute | solution.py:441
  40.2 42.4 %collective-permute-start.5 = (bf16[832,1024]{1,0:T(8,128)(2,1)}, bf16[832,1024]{1,0:T(8,128)(2,1)}, u32[]{:S(2)}, u32[]{:S(2)}) collective-permute-start(bf16[832,1024]{1,0:T(8,128)(2,1)} %shard_map.84.refs_0_), channel_id=1, source_target_pairs={{0,1},{1,0},{2,3},{3,2},{4,5},{5,4},{6,7},{7,6},{8,9},{9,8},{10,11... | collective-permute-start | bytes 5111816 | tf_op jit(solution)/shard_map/ppermute | solution.py:431
  56.2 61.6 %collective-permute-start.4 = (bf16[816,1024]{1,0:T(8,128)(2,1)}, bf16[816,1024]{1,0:T(8,128)(2,1)}, u32[]{:S(2)}, u32[]{:S(2)}) collective-permute-start(bf16[816,1024]{1,0:T(8,128)(2,1)} %shard_map.88.refs_1_), channel_id=1, source_target_pairs={{0,1},{1,0},{2,3},{3,2},{4,5},{5,4},{6,7},{7,6},{8,9},{9,8},{10,11... | collective-permute-start | bytes 5013512 | tf_op jit(solution)/shard_map/ppermute | solution.py:431
  62.0 26.4 %collective-permute-start.8 = (bf16[384,1024]{1,0:T(8,128)(2,1)}, bf16[384,1024]{1,0:T(8,128)(2,1)S(1)}, u32[]{:S(2)}, u32[]{:S(2)}) collective-permute-start(bf16[384,1024]{1,0:T(8,128)(2,1)} %shard_map.89.refs_1_.refs_2_.refs_3_), channel_id=1, source_target_pairs={{0,2},{1,3},{6,4},{7,5},{8,10},{9,11},{14,12},{15,13},{16,18},{17,... | collective-permute-start | bytes 2359304 | tf_op jit(solution)/shard_map/ppermute | solution.py:468
  68.8 19.6 %copy-start.16 = (s32[16]{0:T(128)S(1)}, s32[16]{0:T(128)}, u32[]{:S(2)}) copy-start(s32[16]{0:T(128)} %dynamic-slice_bitcast_fusion.scalars_ref) | copy-start | bytes 196
  68.8 30.8 %collective-permute-start.7 = (bf16[384,1024]{1,0:T(8,128)(2,1)}, bf16[384,1024]{1,0:T(8,128)(2,1)S(1)}, u32[]{:S(2)}, u32[]{:S(2)}) collective-permute-start(bf16[384,1024]{1,0:T(8,128)(2,1)} %shard_map.90.refs_1_.refs_2_.refs_3_), channel_id=1, source_target_pairs={{0,2},{1,3},{6,4},{7,5},{8,10},{9,11},{14,12},{15,13},{16,18},{17,... | collective-permute-start | bytes 2359304 | tf_op jit(solution)/shard_map/ppermute | solution.py:468
  91.3 34.2 %collective-permute-start.11 = (bf16[384,1024]{1,0:T(8,128)(2,1)S(1)}, bf16[384,1024]{1,0:T(8,128)(2,1)S(1)}, u32[]{:S(2)}, u32[]{:S(2)}) collective-permute-start(bf16[384,1024]{1,0:T(8,128)(2,1)S(1)} %shard_map.92.refs_0_), channel_id=1, source_target_pairs={{0,2},{1,3},{2,4},{3,5},{8,10},{9,11},{10,12},{11,13},{16,18},{17,... | collective-permute-start | bytes 2359304 | tf_op jit(solution)/shard_map/ppermute | solution.py:493
  95.4 30.1 %collective-permute-start.12 = (bf16[384,1024]{1,0:T(8,128)(2,1)S(1)}, bf16[384,1024]{1,0:T(8,128)(2,1)S(1)}, u32[]{:S(2)}, u32[]{:S(2)}) collective-permute-start(bf16[384,1024]{1,0:T(8,128)(2,1)S(1)} %shard_map.92.refs_0_), channel_id=1, source_target_pairs={{4,2},{5,3},{6,4},{7,5},{12,10},{13,11},{14,12},{15,13},{20,18},{2... | collective-permute-start | bytes 2359304 | tf_op jit(solution)/shard_map/ppermute | solution.py:493
  100.6 34.6 %collective-permute-start.9 = (bf16[384,1024]{1,0:T(8,128)(2,1)S(1)}, bf16[384,1024]{1,0:T(8,128)(2,1)S(1)}, u32[]{:S(2)}, u32[]{:S(2)}) collective-permute-start(bf16[384,1024]{1,0:T(8,128)(2,1)S(1)} %shard_map.93.refs_0_), channel_id=1, source_target_pairs={{0,2},{1,3},{2,4},{3,5},{8,10},{9,11},{10,12},{11,13},{16,18},{17,... | collective-permute-start | bytes 2359304 | tf_op jit(solution)/shard_map/ppermute | solution.py:493
  105.0 30.3 %collective-permute-start.10 = (bf16[384,1024]{1,0:T(8,128)(2,1)S(1)}, bf16[384,1024]{1,0:T(8,128)(2,1)S(1)}, u32[]{:S(2)}, u32[]{:S(2)}) collective-permute-start(bf16[384,1024]{1,0:T(8,128)(2,1)S(1)} %shard_map.93.refs_0_), channel_id=1, source_target_pairs={{4,2},{5,3},{6,4},{7,5},{12,10},{13,11},{14,12},{15,13},{20,18},{2... | collective-permute-start | bytes 2359304 | tf_op jit(solution)/shard_map/ppermute | solution.py:493
  111.0 14.4 %copy-start.4 = (bf16[384,1024]{1,0:T(8,128)(2,1)S(1)}, bf16[384,1024]{1,0:T(8,128)(2,1)}, u32[]{:S(2)}) copy-start(bf16[384,1024]{1,0:T(8,128)(2,1)} %shard_map.89.refs_1_.refs_2_.refs_3_) | copy-start | bytes 2359300
  111.0 14.5 %copy-start.17 = (s32[16]{0:T(128)S(1)}, s32[16]{0:T(128)}, u32[]{:S(2)}) copy-start(s32[16]{0:T(128)} %dynamic-slice_bitcast_fusion.scalars_ref) | copy-start | bytes 196
  117.7 43.5 %collective-permute-start.13 = (bf16[768,1024]{1,0:T(8,128)(2,1)}, bf16[768,1024]{1,0:T(8,128)(2,1)}, u32[]{:S(2)}, u32[]{:S(2)}) collective-permute-start(bf16[768,1024]{1,0:T(8,128)(2,1)} %shard_map.94.refs_1_), channel_id=1, source_target_pairs={{0,1},{1,0},{2,3},{3,2},{4,5},{5,4},{6,7},{7,6},{8,9},{9,8},{10,11... | collective-permute-start | bytes 4718600 | tf_op jit(solution)/shard_map/ppermute | solution.py:431
  119.5 15.8 %copy-start.5 = (bf16[384,1024]{1,0:T(8,128)(2,1)S(1)}, bf16[384,1024]{1,0:T(8,128)(2,1)}, u32[]{:S(2)}) copy-start(bf16[384,1024]{1,0:T(8,128)(2,1)} %shard_map.90.refs_1_.refs_2_.refs_3_) | copy-start | bytes 2359300
  129.6 31.7 %collective-permute-start.14 = (bf16[384,1024]{1,0:T(8,128)(2,1)}, bf16[384,1024]{1,0:T(8,128)(2,1)}, u32[]{:S(2)}, u32[]{:S(2)}) collective-permute-start(bf16[384,1024]{1,0:T(8,128)(2,1)} %get-tuple-element.21.refs_4_), channel_id=1, source_target_pairs={{0,2},{1,3},{2,4},{3,5},{4,6},{5,7},{8,10},{9,11},{10,12},{11,13},... | collective-permute-start | bytes 2359304 | tf_op jit(solution)/shard_map/ppermute | solution.py:493
  133.9 27.3 %collective-permute-start.15 = (bf16[384,1024]{1,0:T(8,128)(2,1)}, bf16[384,1024]{1,0:T(8,128)(2,1)}, u32[]{:S(2)}, u32[]{:S(2)}) collective-permute-start(bf16[384,1024]{1,0:T(8,128)(2,1)} %get-tuple-element.23), channel_id=1, source_target_pairs={{2,0},{3,1},{4,2},{5,3},{6,4},{7,5},{10,8},{11,9},{12,10},{13,11},... | collective-permute-start | bytes 2359304 | tf_op jit(solution)/shard_map/ppermute | solution.py:493
  135.2 13.5 %copy-start.3 = (f32[768,1024]{1,0:T(8,128)S(1)}, f32[768,1024]{1,0:T(8,128)}, u32[]{:S(2)}) copy-start(f32[768,1024]{1,0:T(8,128)} %shard_map.86.refs_0_.rest_ref) | copy-start | bytes 9437188
  137.5 28.5 %collective-permute-start.16 = (bf16[384,1024]{1,0:T(8,128)(2,1)}, bf16[384,1024]{1,0:T(8,128)(2,1)}, u32[]{:S(2)}, u32[]{:S(2)}) collective-permute-start(bf16[384,1024]{1,0:T(8,128)(2,1)} %get-tuple-element.22.refs_0_), channel_id=1, source_target_pairs={{0,2},{1,3},{2,4},{3,5},{4,6},{5,7},{8,10},{9,11},{10,12},{11,13},... | collective-permute-start | bytes 2359304 | tf_op jit(solution)/shard_map/ppermute | solution.py:493
  143.0 28.0 %collective-permute-start.17 = (bf16[384,1024]{1,0:T(8,128)(2,1)}, bf16[384,1024]{1,0:T(8,128)(2,1)}, u32[]{:S(2)}, u32[]{:S(2)}) collective-permute-start(bf16[384,1024]{1,0:T(8,128)(2,1)} %get-tuple-element.24), channel_id=1, source_target_pairs={{2,0},{3,1},{4,2},{5,3},{6,4},{7,5},{10,8},{11,9},{12,10},{13,11},... | collective-permute-start | bytes 2359304 | tf_op jit(solution)/shard_map/ppermute | solution.py:493
  (15 other events, 46.3 us)

commit v3 on v2

--- a/solution.py
+++ b/solution.py
@@ -14,7 +14,7 @@
 
 
 def params(large=False):
-    return pltpu.CompilerParams(vmem_limit_bytes=(56 if large else 32) * 2**20)
+    return pltpu.CompilerParams(vmem_limit_bytes=(56 if large else 48) * 2**20)
 
 
 def line_plan(places):
@@ -234,6 +234,34 @@
         pl.BlockSpec((tile, bank.shape[1]), lambda j: (jnp.minimum(j, half - 1), 0)),
         pl.BlockSpec((tile, bank.shape[1]), lambda j: (jnp.maximum(j - half, 0), 0)),
     ]
+
+
+def rows_body(added, *refs):
+    total = refs[0][...].astype(F32)
+    for ref in refs[1:added]:
+        total = total + ref[...].astype(F32)
+    refs[-1][...] = total
+
+
+def cut_spec(array, rows, tile, block):
+    if array.shape[0] == rows:
+        return pl.BlockSpec((rows, tile), lambda j, *s: (0, j))
+    return pl.BlockSpec((rows, tile), lambda j, *s: (block, j))
+
+
+def add_rows(values, rows, block, after=()):
+    width = values[0].shape[1]
+    tile = min(512, width)
+    return pl.pallas_call(
+        functools.partial(rows_body, len(values)),
+        out_shape=jax.ShapeDtypeStruct((rows, width), F32),
+        grid=(width // tile,),
+        in_specs=[cut_spec(v, rows, tile, block) for v in values]
+        + [pl.BlockSpec(memory_space=pl.ANY)] * len(after),
+        out_specs=pl.BlockSpec((rows, tile), lambda j: (0, j)),
+        compiler_params=params(),
+        cost_estimate=SMALL,
+    )(*values, *after)
 
 
 def shrink_body(rank, slot_ref, x_ref, own_ref, other_ref, *refs):
@@ -457,9 +485,7 @@
             last = send_along_y(s + 1, last)
         parts = []
         if s > 1:
-            last = whole = product(
-                x, weight, scalars, here_at[k], width, (y_got[k],), after=(last,), dtype=F32
-            )
+            last = whole = add_rows((mine, y_got[k]), rows, 0, after=(last,))
         for b in range(blocks):
             if s == 1:
                 last = product(
@@ -492,6 +518,8 @@
                 last = outs[0]
             arrived[b] = lax.ppermute(outs[0], "tensor", ups), lax.ppermute(outs[1], "tensor", downs)
         values.append(parts)
+        if s < final:
+            last = mine = product(x, weight, scalars, here_at[s], width, after=(last,), dtype=F32)
         if 1 < s < final:
             last = send_along_y(s + 1, last)
 

time: 176 us -> 174 us (0.989)
  Pallas kernels: 78.4 us -> 87.4 us
  local copies, waits for them, and re-layouts: 18.6 us -> 11.6 us
  other arithmetic: 2.75 us -> 0.17 us
    ppermute x3, waiting for transfers between devices: 19 us -> 12.3 us  [send_along_y(): y_got.append(lax.ppermute(sent, 'tensor', swap_y))]
    pallas_call x0 -> x2, Pallas kernels: none -> 5.45 us  [add_rows(): pl.pallas_call(functools.partial(rows_body, len(values)), out_shape=jax.S...]
    unnamed x42 -> x36, local copies, waits for them, and re-layouts: 14.9 us -> 9.54 us
    ppermute x2, waiting for transfers between devices: 3.57 us -> 6.44 us  [shards(): arrived[b] = (lax.ppermute(last, 'tensor', ups + downs),)]
    ppermute x4, waiting for transfers between devices: 4.75 us -> 6.95 us  [shards(): lax.ppermute(outs[0], 'tensor', ups)]
  transfers between devices with their start and end apart: 18 -> 18, of which waited for: 6 -> 6; matrix products, arithmetic and copies ran while one was open for 4% -> 1% of each run, Pallas kernels for 43% -> 48%
where the time goes in v3:
time: 174 us; the launch traced here: 173 us
  Pallas kernels  87.4 us (50%)
  starting transfers between devices  39.2 us (23%)
  waiting for transfers between devices  33.9 us (19%)
  local copies, waits for them, and re-layouts  11.6 us (7%)
    pallas_call x8, Pallas kernels, product(): pl.pallas_call(functools.partial(product_body, len(adds), more), out_shap...  41.6 us
    ppermute x4, starting transfers between devices, shards(): lax.ppermute(outs[0], 'tensor', ups)  18.2 us
    ppermute x3, waiting for transfers between devices, send_along_y(): y_got.append(lax.ppermute(sent, 'tensor', swap_y))  12.3 us
    pallas_call x1, Pallas kernels, expand_rows(): pl.pallas_call(functools.partial(expand_body, rank), out_shape=jax.ShapeD...  12 us
    pallas_call x1, Pallas kernels, shrink_rows(): pl.pallas_call(functools.partial(shrink_body, rank), out_shape=jax.ShapeD...  10.7 us
    unnamed x36, local copies, waits for them, and re-layouts  9.54 us
    pallas_call x4, Pallas kernels, sums(): pl.pallas_call(functools.partial(sums_body, column, count) if count else...  7.9 us
    ppermute x4, waiting for transfers between devices, shards(): lax.ppermute(outs[0], 'tensor', ups)  6.95 us
  transfers between devices with their start and end apart: 18, of which 6 were waited for; matrix products, arithmetic and copies ran while one was open for 1% of the time, Pallas kernels for 48%

profile of v3, /device:TPU:0, one launch (start us, length us, event | category | flops | bytes accessed | tf_op | source)
XLA Modules:
  0.0 172.6 jit_solution(12855216848342854678)
XLA Ops:
  1.7 5.8 %shard_map.82 = (bf16[768,1024]{1,0:T(8,128)(2,1)}, bf16[768,1024]{1,0:T(8,128)(2,1)}) custom-call(s32[16]{0:T(128)} %dynamic-slice_bitcast_fusion.scalars_ref, bf16[768,1024]{1,0:T(8,128)(2,1)} %x_ref.1, f32[1,1024]{1,0:T(1,128)} %bitcast.9, bf16[1024,8192]{1,0:T(8,128)(2,1)} %w_ref.17), custom_call_target="tpu_custom_call" | custom-call | flops 1 | bytes 1 | tf_op jit(solution)/shard_map/pallas_call | solution.py:73
  15.2 10.7 %shard_map.83.refs_1_.total_ref = f32[384,128]{1,0:T(8,128)S(1)} custom-call(s32[768,128]{1,0:T(8,128)S(1)} %broadcast_in_dim.2.slot_ref, bf16[768,1024]{1,0:T(8,128)(2,1)S(1)} %copy-done.5, bf16[2048,1024]{1,0:T(8,128)(2,1)} %bitcast.6, bf16[2048,1024]{1,0:T(8,128)(2,1)} %collective-permute-done.other_ref, bf16[768,1024]{1,0:T(8,128)(2,1)S(1)} %copy-done.9, ...), custom_call_target="tpu_custom_call" | custom-call | flops 1 | bytes 1 | tf_op jit(solution)/shard_map/pallas_call | solution.py:301
  25.9 3.0 %collective-permute-start.2 = (bf16[384,128]{1,0:T(8,128)(2,1)S(1)}, bf16[384,128]{1,0:T(8,128)(2,1)S(1)}, u32[]{:S(2)}, u32[]{:S(2)}) collective-permute-start(bf16[384,128]{1,0:T(8,128)(2,1)S(1)} %convert_element_type.13), channel_id=1, source_target_pairs={{0,2},{1,3},{2,0},{3,1},{4,6},{5,7},{6,4},{7,5},{8,10},{9,11},{10,... | collective-permute-start | bytes 294920 | tf_op jit(solution)/shard_map/ppermute | solution.py:469
  28.9 5.3 %shard_map.84.refs_0_ = bf16[832,1024]{1,0:T(8,128)(2,1)} custom-call(s32[16]{0:T(128)} %dynamic-slice_bitcast_fusion.scalars_ref, bf16[768,1024]{1,0:T(8,128)(2,1)} %get-tuple-element.16.x_ref.refs_0_, bf16[1024,8192]{1,0:T(8,128)(2,1)} %w_ref.17, bf16[768,1024]{1,0:T(8,128)(2,1)} %get-tuple-element.16.x_ref.refs_0_, f32[384,128]{1,0:T(8,128)} %copy-done.6), custom_call_target="tpu_custom_call" | custom-call | flops 1 | bytes 1 | tf_op jit(solution)/shard_map/pallas_call | solution.py:190
  40.0 5.7 %shard_map.86.refs_0_.rest_ref = f32[768,1024]{1,0:T(8,128)} custom-call(s32[16]{0:T(128)} %dynamic-slice_bitcast_fusion.scalars_ref, bf16[768,1024]{1,0:T(8,128)(2,1)} %get-tuple-element.16.x_ref.refs_0_, bf16[1024,8192]{1,0:T(8,128)(2,1)} %w_ref.17, f32[384,128]{1,0:T(8,128)} %copy-done.12), custom_call_target="tpu_custom_call" | custom-call | flops 1 | bytes 1 | tf_op jit(solution)/shard_map/pallas_call | solution.py:190
  49.0 5.4 %shard_map.88.refs_1_ = bf16[816,1024]{1,0:T(8,128)(2,1)} custom-call(s32[16]{0:T(128)} %dynamic-slice_bitcast_fusion.scalars_ref, bf16[768,1024]{1,0:T(8,128)(2,1)} %get-tuple-element.16.x_ref.refs_0_, bf16[1024,8192]{1,0:T(8,128)(2,1)} %w_ref.17, bf16[48,1024]{1,0:T(8,128)(2,1)} %reshape.29.refs_0_, f32[384,128]{1,0:T(8,128)} %copy-done.10), custom_call_target="tpu_custom_call" | custom-call | flops 1 | bytes 1 | tf_op jit(solution)/shard_map/pallas_call | solution.py:190
  54.9 4.2 %shard_map.89.refs_1_.refs_2_.refs_3_ = bf16[384,1024]{1,0:T(8,128)(2,1)} custom-call(s32[16]{0:T(128)} %dynamic-slice_bitcast_fusion.scalars_ref, bf16[768,1024]{1,0:T(8,128)(2,1)} %get-tuple-element.16.x_ref.refs_0_, bf16[1024,8192]{1,0:T(8,128)(2,1)} %w_ref.17, bf16[768,1024]{1,0:T(8,128)(2,1)} %collective-permute-done.5.refs_0_, ...), custom_call_target="tpu_custom_call" | custom-call | flops 1 | bytes 1 | tf_op jit(solution)/shard_map/pallas_call | solution.py:190
  61.7 4.2 %shard_map.90.refs_0_.refs_2_.refs_3_ = bf16[384,1024]{1,0:T(8,128)(2,1)} custom-call(s32[16]{0:T(128)} %dynamic-slice_bitcast_fusion.scalars_ref, bf16[768,1024]{1,0:T(8,128)(2,1)} %get-tuple-element.16.x_ref.refs_0_, bf16[1024,8192]{1,0:T(8,128)(2,1)} %w_ref.17, bf16[768,1024]{1,0:T(8,128)(2,1)} %collective-permute-done.5.refs_0_, ...), custom_call_target="tpu_custom_call" | custom-call | flops 1 | bytes 1 | tf_op jit(solution)/shard_map/pallas_call | solution.py:190
  67.3 5.7 %shard_map.91.refs_0_.refs_2_ = f32[768,1024]{1,0:T(8,128)} custom-call(s32[16]{0:T(128)} %dynamic-slice_bitcast_fusion.scalars_ref, bf16[768,1024]{1,0:T(8,128)(2,1)} %get-tuple-element.16.x_ref.refs_0_, bf16[1024,8192]{1,0:T(8,128)(2,1)} %w_ref.17, bf16[384,1024]{1,0:T(8,128)(2,1)} %shard_map.90.refs_0_.refs_2_.refs_3_), custom_call_target="tpu_custom_call" | custom-call | flops 1 | bytes 1 | tf_op jit(solution)/shard_map/pallas_call | solution.py:190
  72.9 9.4 %collective-permute-done.6.refs_1_ = bf16[832,1024]{1,0:T(8,128)(2,1)S(1)} collective-permute-done((bf16[832,1024]{1,0:T(8,128)(2,1)}, bf16[832,1024]{1,0:T(8,128)(2,1)S(1)}, u32[]{:S(2)}, u32[]{:S(2)}) %collective-permute-start.6) | collective-permute-done | bytes 1703968 | tf_op jit(solution)/shard_map/ppermute | solution.py:459
  85.5 4.1 %collective-permute-start.11 = (bf16[384,1024]{1,0:T(8,128)(2,1)S(1)}, bf16[384,1024]{1,0:T(8,128)(2,1)S(1)}, u32[]{:S(2)}, u32[]{:S(2)}) collective-permute-start(bf16[384,1024]{1,0:T(8,128)(2,1)S(1)} %shard_map.93.refs_0_), channel_id=1, source_target_pairs={{0,2},{1,3},{2,4},{3,5},{8,10},{9,11},{10,12},{11,13},{16,18},{17,... | collective-permute-start | bytes 2359304 | tf_op jit(solution)/shard_map/ppermute | solution.py:519
  90.3 6.4 %collective-permute-done.7.got_ref = bf16[384,1024]{1,0:T(8,128)(2,1)S(1)} collective-permute-done((bf16[384,1024]{1,0:T(8,128)(2,1)}, bf16[384,1024]{1,0:T(8,128)(2,1)S(1)}, u32[]{:S(2)}, u32[]{:S(2)}) %collective-permute-start.7) | collective-permute-done | bytes 786464 | tf_op jit(solution)/shard_map/ppermute | solution.py:494
  98.6 5.6 %shard_map.95.refs_0_ = f32[768,1024]{1,0:T(8,128)} custom-call(s32[16]{0:T(128)} %dynamic-slice_bitcast_fusion.scalars_ref, bf16[768,1024]{1,0:T(8,128)(2,1)} %get-tuple-element.16.x_ref.refs_0_, bf16[1024,8192]{1,0:T(8,128)(2,1)} %w_ref.17, bf16[384,1024]{1,0:T(8,128)(2,1)} %copy-done.8), custom_call_target="tpu_custom_call" | custom-call | flops 1 | bytes 1 | tf_op jit(solution)/shard_map/pallas_call | solution.py:190
  104.2 4.3 %collective-permute-start.9 = (bf16[384,1024]{1,0:T(8,128)(2,1)}, bf16[384,1024]{1,0:T(8,128)(2,1)S(1)}, u32[]{:S(2)}, u32[]{:S(2)}) collective-permute-start(bf16[384,1024]{1,0:T(8,128)(2,1)} %copy-done.8), channel_id=1, source_target_pairs={{0,2},{1,3},{2,4},{3,5},{8,10},{9,11},{10,12},{11,13},{16,18},{17,... | collective-permute-start | bytes 2359304 | tf_op jit(solution)/shard_map/ppermute | solution.py:519
  109.3 5.4 %shard_map.96.refs_2_ = bf16[768,1024]{1,0:T(8,128)(2,1)} custom-call(s32[16]{0:T(128)} %dynamic-slice_bitcast_fusion.scalars_ref, bf16[768,1024]{1,0:T(8,128)(2,1)} %get-tuple-element.16.x_ref.refs_0_, bf16[1024,8192]{1,0:T(8,128)(2,1)} %w_ref.17, f32[768,1024]{1,0:T(8,128)} %shard_map.95.refs_0_), custom_call_target="tpu_custom_call" | custom-call | flops 1 | bytes 1 | tf_op jit(solution)/shard_map/pallas_call | solution.py:190
  120.7 3.3 %shard_map.97.sum_ref.refs_4_ = f32[768,1024]{1,0:T(8,128)} custom-call(f32[768,1024]{1,0:T(8,128)} %shard_map.95.refs_0_, bf16[816,1024]{1,0:T(8,128)(2,1)S(1)} %collective-permute-done.4.refs_1_, bf16[768,1024]{1,0:T(8,128)(2,1)S(1)} %copy-done.4), custom_call_target="tpu_custom_call" | custom-call | flops 1 | bytes 1 | tf_op jit(solution)/shard_map/pallas_call | solution.py:255
  124.1 3.0 %shard_map.98 = (bf16[384,1024]{1,0:T(8,128)(2,1)}, bf16[384,1024]{1,0:T(8,128)(2,1)}) custom-call(s32[16]{0:T(128)S(1)} %copy-done.15, f32[768,1024]{1,0:T(8,128)} %shard_map.97.sum_ref.refs_4_, bf16[384,1024]{1,0:T(8,128)(2,1)S(1)} %collective-permute-done.11.refs_0_, bf16[384,1024]{1,0:T(8,128)(2,1)S(1)} %collective-permute-done.12.refs_1_, ...), custom_call_target="tpu_custom_call" | custom-call | flops 1 | bytes 1 | tf_op jit(solution)/shard_map/pallas_call | solution.py:146
  127.1 4.3 %collective-permute-start.14 = (bf16[384,1024]{1,0:T(8,128)(2,1)}, bf16[384,1024]{1,0:T(8,128)(2,1)}, u32[]{:S(2)}, u32[]{:S(2)}) collective-permute-start(bf16[384,1024]{1,0:T(8,128)(2,1)} %get-tuple-element.21.refs_4_), channel_id=1, source_target_pairs={{0,2},{1,3},{2,4},{3,5},{4,6},{5,7},{8,10},{9,11},{10,12},{11,13},... | collective-permute-start | bytes 2359304 | tf_op jit(solution)/shard_map/ppermute | solution.py:519
  132.9 3.0 %shard_map.99 = (bf16[384,1024]{1,0:T(8,128)(2,1)S(1)}, bf16[384,1024]{1,0:T(8,128)(2,1)}) custom-call(s32[16]{0:T(128)S(1)} %copy-done.15, f32[768,1024]{1,0:T(8,128)} %shard_map.97.sum_ref.refs_4_, bf16[384,1024]{1,0:T(8,128)(2,1)S(1)} %collective-permute-done.9.refs_0_, bf16[384,1024]{1,0:T(8,128)(2,1)S(1)} %collective-permute-done.10.refs_1_, ...), custom_call_target="tpu_custom_call" | custom-call | flops 1 | bytes 1 | tf_op jit(solution)/shard_map/pallas_call | solution.py:146
  135.9 5.4 %collective-permute-start.16 = (bf16[384,1024]{1,0:T(8,128)(2,1)S(1)}, bf16[384,1024]{1,0:T(8,128)(2,1)}, u32[]{:S(2)}, u32[]{:S(2)}) collective-permute-start(bf16[384,1024]{1,0:T(8,128)(2,1)S(1)} %get-tuple-element.22.refs_0_), channel_id=1, source_target_pairs={{0,2},{1,3},{2,4},{3,5},{4,6},{5,7},{8,10},{9,11},{10,12},{11,13},... | collective-permute-start | bytes 2359304 | tf_op jit(solution)/shard_map/ppermute | solution.py:519
  142.9 12.0 %shard_map.100.base_ref = f32[768,1024]{1,0:T(8,128)S(1)} custom-call(s32[768,128]{1,0:T(8,128)S(1)} %broadcast_in_dim.2.slot_ref, bf16[384,128]{1,0:T(8,128)(2,1)S(1)} %add_convert_fusion.shrunk_ref, bf16[2048,1024]{1,0:T(8,128)(2,1)} %bitcast.8, bf16[2048,1024]{1,0:T(8,128)(2,1)} %collective-permute-done.1.refs_1_.other_ref, ...), custom_call_target="tpu_custom_call" | custom-call | flops 1 | bytes 1 | tf_op jit(solution)/shard_map/pallas_call | solution.py:356
  156.5 6.9 %collective-permute-done.16.refs_2_ = bf16[384,1024]{1,0:T(8,128)(2,1)} collective-permute-done((bf16[384,1024]{1,0:T(8,128)(2,1)S(1)}, bf16[384,1024]{1,0:T(8,128)(2,1)}, u32[]{:S(2)}, u32[]{:S(2)}) %collective-permute-start.16) | collective-permute-done | bytes 786464 | tf_op jit(solution)/shard_map/ppermute | solution.py:519
  163.4 5.2 %collective-permute-done.17.refs_3_ = bf16[384,1024]{1,0:T(8,128)(2,1)} collective-permute-done((bf16[384,1024]{1,0:T(8,128)(2,1)}, bf16[384,1024]{1,0:T(8,128)(2,1)}, u32[]{:S(2)}, u32[]{:S(2)}) %collective-permute-start.17) | collective-permute-done | bytes 786464 | tf_op jit(solution)/shard_map/ppermute | solution.py:519
  168.6 4.0 %shard_map.101 = bf16[768,1024]{1,0:T(8,128)(2,1)} custom-call(f32[768,1024]{1,0:T(8,128)} %copy-done.3, bf16[768,1024]{1,0:T(8,128)(2,1)S(1)} %collective-permute-done.13.y_ref, bf16[384,1024]{1,0:T(8,128)(2,1)} %collective-permute-done.14.refs_0_, bf16[384,1024]{1,0:T(8,128)(2,1)} %collective-permute-done.15.refs_1_, ...), custom_call_target="tpu_custom_call" | custom-call | flops 1 | bytes 1 | tf_op jit(solution)/shard_map/pallas_call | solution.py:385
  (78 shorter events, 39.8 us)
Async XLA Ops:
  0.0 10.6 %collective-permute-start = (bf16[2048,1024]{1,0:T(8,128)(2,1)}, bf16[2048,1024]{1,0:T(8,128)(2,1)}, u32[]{:S(2)}, u32[]{:S(2)}) collective-permute-start(bf16[2048,1024]{1,0:T(8,128)(2,1)} %bitcast.5), channel_id=1, source_target_pairs={{0,8},{8,0},{1,9},{9,1},{2,10},{10,2},{3,11},{11,3},{4,12},{12,4},... | collective-permute-start | bytes 12582920 | tf_op jit(solution)/shard_map/ppermute | solution.py:440
  0.5 13.1 %collective-permute-start.1 = (bf16[2048,1024]{1,0:T(8,128)(2,1)}, bf16[2048,1024]{1,0:T(8,128)(2,1)}, u32[]{:S(2)}, u32[]{:S(2)}) collective-permute-start(bf16[2048,1024]{1,0:T(8,128)(2,1)} %bitcast.7), channel_id=1, source_target_pairs={{0,8},{8,0},{1,9},{9,1},{2,10},{10,2},{3,11},{11,3},{4,12},{12,4},... | collective-permute-start | bytes 12582920 | tf_op jit(solution)/shard_map/ppermute | solution.py:441
  1.7 12.0 %copy-start.5 = (bf16[768,1024]{1,0:T(8,128)(2,1)S(1)}, bf16[768,1024]{1,0:T(8,128)(2,1)}, u32[]{:S(2)}) copy-start(bf16[768,1024]{1,0:T(8,128)(2,1)} %x_ref.1) | copy-start | bytes 4718596
  7.5 47.5 %collective-permute-start.5 = (bf16[768,1024]{1,0:T(8,128)(2,1)}, bf16[768,1024]{1,0:T(8,128)(2,1)}, u32[]{:S(2)}, u32[]{:S(2)}) collective-permute-start(bf16[768,1024]{1,0:T(8,128)(2,1)} %get-tuple-element.15.refs_0_), channel_id=1, source_target_pairs={{0,1},{1,0},{2,3},{3,2},{4,5},{5,4},{6,7},{7,6},{8,9},{9,8},{10,11... | collective-permute-start | bytes 4718600 | tf_op jit(solution)/shard_map/ppermute | solution.py:463
  25.9 8.4 %collective-permute-start.2 = (bf16[384,128]{1,0:T(8,128)(2,1)S(1)}, bf16[384,128]{1,0:T(8,128)(2,1)S(1)}, u32[]{:S(2)}, u32[]{:S(2)}) collective-permute-start(bf16[384,128]{1,0:T(8,128)(2,1)S(1)} %convert_element_type.13), channel_id=1, source_target_pairs={{0,2},{1,3},{2,0},{3,1},{4,6},{5,7},{6,4},{7,5},{8,10},{9,11},{10,... | collective-permute-start | bytes 294920 | tf_op jit(solution)/shard_map/ppermute | solution.py:469
  35.9 9.9 %collective-permute-start.3 = (bf16[384,128]{1,0:T(8,128)(2,1)S(1)}, bf16[384,128]{1,0:T(8,128)(2,1)S(1)}, u32[]{:S(2)}, u32[]{:S(2)}) collective-permute-start(bf16[384,128]{1,0:T(8,128)(2,1)S(1)} %get-tuple-element.18), channel_id=1, source_target_pairs={{0,4},{1,5},{2,6},{3,7},{4,0},{5,1},{6,2},{7,3},{8,12},{9,13},{10,... | collective-permute-start | bytes 294920 | tf_op jit(solution)/shard_map/ppermute | solution.py:469
  38.5 43.9 %collective-permute-start.6 = (bf16[832,1024]{1,0:T(8,128)(2,1)}, bf16[832,1024]{1,0:T(8,128)(2,1)S(1)}, u32[]{:S(2)}, u32[]{:S(2)}) collective-permute-start(bf16[832,1024]{1,0:T(8,128)(2,1)} %shard_map.84.refs_0_), channel_id=1, source_target_pairs={{0,1},{1,0},{2,3},{3,2},{4,5},{5,4},{6,7},{7,6},{8,9},{9,8},{10,11... | collective-permute-start | bytes 5111816 | tf_op jit(solution)/shard_map/ppermute | solution.py:459
  54.4 63.1 %collective-permute-start.4 = (bf16[816,1024]{1,0:T(8,128)(2,1)}, bf16[816,1024]{1,0:T(8,128)(2,1)S(1)}, u32[]{:S(2)}, u32[]{:S(2)}) collective-permute-start(bf16[816,1024]{1,0:T(8,128)(2,1)} %shard_map.88.refs_1_), channel_id=1, source_target_pairs={{0,1},{1,0},{2,3},{3,2},{4,5},{5,4},{6,7},{7,6},{8,9},{9,8},{10,11... | collective-permute-start | bytes 5013512 | tf_op jit(solution)/shard_map/ppermute | solution.py:459
  59.1 25.4 %collective-permute-start.8 = (bf16[384,1024]{1,0:T(8,128)(2,1)}, bf16[384,1024]{1,0:T(8,128)(2,1)S(1)}, u32[]{:S(2)}, u32[]{:S(2)}) collective-permute-start(bf16[384,1024]{1,0:T(8,128)(2,1)} %shard_map.89.refs_1_.refs_2_.refs_3_), channel_id=1, source_target_pairs={{0,2},{1,3},{6,4},{7,5},{8,10},{9,11},{14,12},{15,13},{16,18},{17,... | collective-permute-start | bytes 2359304 | tf_op jit(solution)/shard_map/ppermute | solution.py:494
  65.9 30.9 %collective-permute-start.7 = (bf16[384,1024]{1,0:T(8,128)(2,1)}, bf16[384,1024]{1,0:T(8,128)(2,1)S(1)}, u32[]{:S(2)}, u32[]{:S(2)}) collective-permute-start(bf16[384,1024]{1,0:T(8,128)(2,1)} %shard_map.90.refs_0_.refs_2_.refs_3_), channel_id=1, source_target_pairs={{0,2},{1,3},{6,4},{7,5},{8,10},{9,11},{14,12},{15,13},{16,18},{17,... | collective-permute-start | bytes 2359304 | tf_op jit(solution)/shard_map/ppermute | solution.py:494
  72.9 11.6 %copy-start.14 = (s32[16]{0:T(128)S(1)}, s32[16]{0:T(128)}, u32[]{:S(2)}) copy-start(s32[16]{0:T(128)} %dynamic-slice_bitcast_fusion.scalars_ref) | copy-start | bytes 196
  85.5 38.5 %collective-permute-start.11 = (bf16[384,1024]{1,0:T(8,128)(2,1)S(1)}, bf16[384,1024]{1,0:T(8,128)(2,1)S(1)}, u32[]{:S(2)}, u32[]{:S(2)}) collective-permute-start(bf16[384,1024]{1,0:T(8,128)(2,1)S(1)} %shard_map.93.refs_0_), channel_id=1, source_target_pairs={{0,2},{1,3},{2,4},{3,5},{8,10},{9,11},{10,12},{11,13},{16,18},{17,... | collective-permute-start | bytes 2359304 | tf_op jit(solution)/shard_map/ppermute | solution.py:519
  89.6 34.4 %collective-permute-start.12 = (bf16[384,1024]{1,0:T(8,128)(2,1)S(1)}, bf16[384,1024]{1,0:T(8,128)(2,1)S(1)}, u32[]{:S(2)}, u32[]{:S(2)}) collective-permute-start(bf16[384,1024]{1,0:T(8,128)(2,1)S(1)} %shard_map.93.refs_0_), channel_id=1, source_target_pairs={{4,2},{5,3},{6,4},{7,5},{12,10},{13,11},{14,12},{15,13},{20,18},{2... | collective-permute-start | bytes 2359304 | tf_op jit(solution)/shard_map/ppermute | solution.py:519
  104.2 28.6 %collective-permute-start.9 = (bf16[384,1024]{1,0:T(8,128)(2,1)}, bf16[384,1024]{1,0:T(8,128)(2,1)S(1)}, u32[]{:S(2)}, u32[]{:S(2)}) collective-permute-start(bf16[384,1024]{1,0:T(8,128)(2,1)} %copy-done.8), channel_id=1, source_target_pairs={{0,2},{1,3},{2,4},{3,5},{8,10},{9,11},{10,12},{11,13},{16,18},{17,... | collective-permute-start | bytes 2359304 | tf_op jit(solution)/shard_map/ppermute | solution.py:519
  108.5 24.3 %collective-permute-start.10 = (bf16[384,1024]{1,0:T(8,128)(2,1)}, bf16[384,1024]{1,0:T(8,128)(2,1)S(1)}, u32[]{:S(2)}, u32[]{:S(2)}) collective-permute-start(bf16[384,1024]{1,0:T(8,128)(2,1)} %copy-done.8), channel_id=1, source_target_pairs={{4,2},{5,3},{6,4},{7,5},{12,10},{13,11},{14,12},{15,13},{20,18},{2... | collective-permute-start | bytes 2359304 | tf_op jit(solution)/shard_map/ppermute | solution.py:519
  109.2 14.8 %copy-start.15 = (s32[16]{0:T(128)S(1)}, s32[16]{0:T(128)}, u32[]{:S(2)}) copy-start(s32[16]{0:T(128)} %dynamic-slice_bitcast_fusion.scalars_ref) | copy-start | bytes 196
  114.6 9.4 %copy-start.2 = (bf16[384,1024]{1,0:T(8,128)(2,1)S(1)}, bf16[384,1024]{1,0:T(8,128)(2,1)}, u32[]{:S(2)}) copy-start(bf16[384,1024]{1,0:T(8,128)(2,1)} %shard_map.89.refs_1_.refs_2_.refs_3_) | copy-start | bytes 2359300
  117.6 38.9 %collective-permute-start.13 = (bf16[768,1024]{1,0:T(8,128)(2,1)}, bf16[768,1024]{1,0:T(8,128)(2,1)S(1)}, u32[]{:S(2)}, u32[]{:S(2)}) collective-permute-start(bf16[768,1024]{1,0:T(8,128)(2,1)} %shard_map.96.refs_2_), channel_id=1, source_target_pairs={{0,1},{1,0},{2,3},{3,2},{4,5},{5,4},{6,7},{7,6},{8,9},{9,8},{10,11... | collective-permute-start | bytes 4718600 | tf_op jit(solution)/shard_map/ppermute | solution.py:459
  124.0 8.8 %copy-start.1 = (bf16[384,1024]{1,0:T(8,128)(2,1)S(1)}, bf16[384,1024]{1,0:T(8,128)(2,1)}, u32[]{:S(2)}) copy-start(bf16[384,1024]{1,0:T(8,128)(2,1)} %shard_map.90.refs_0_.refs_2_.refs_3_) | copy-start | bytes 2359300
  127.1 29.4 %collective-permute-start.14 = (bf16[384,1024]{1,0:T(8,128)(2,1)}, bf16[384,1024]{1,0:T(8,128)(2,1)}, u32[]{:S(2)}, u32[]{:S(2)}) collective-permute-start(bf16[384,1024]{1,0:T(8,128)(2,1)} %get-tuple-element.21.refs_4_), channel_id=1, source_target_pairs={{0,2},{1,3},{2,4},{3,5},{4,6},{5,7},{8,10},{9,11},{10,12},{11,13},... | collective-permute-start | bytes 2359304 | tf_op jit(solution)/shard_map/ppermute | solution.py:519
  131.4 11.4 %copy-start.11 = (f32[384,128]{1,0:T(8,128)S(1)}, f32[384,128]{1,0:T(8,128)}, u32[]{:S(2)}) copy-start(f32[384,128]{1,0:T(8,128)} %copy-done.10) | copy-start | bytes 589828
  131.4 25.1 %collective-permute-start.15 = (bf16[384,1024]{1,0:T(8,128)(2,1)}, bf16[384,1024]{1,0:T(8,128)(2,1)}, u32[]{:S(2)}, u32[]{:S(2)}) collective-permute-start(bf16[384,1024]{1,0:T(8,128)(2,1)} %get-tuple-element.23), channel_id=1, source_target_pairs={{2,0},{3,1},{4,2},{5,3},{6,4},{7,5},{10,8},{11,9},{12,10},{13,11},... | collective-permute-start | bytes 2359304 | tf_op jit(solution)/shard_map/ppermute | solution.py:519
  135.9 27.5 %collective-permute-start.16 = (bf16[384,1024]{1,0:T(8,128)(2,1)S(1)}, bf16[384,1024]{1,0:T(8,128)(2,1)}, u32[]{:S(2)}, u32[]{:S(2)}) collective-permute-start(bf16[384,1024]{1,0:T(8,128)(2,1)S(1)} %get-tuple-element.22.refs_0_), channel_id=1, source_target_pairs={{0,2},{1,3},{2,4},{3,5},{4,6},{5,7},{8,10},{9,11},{10,12},{11,13},... | collective-permute-start | bytes 2359304 | tf_op jit(solution)/shard_map/ppermute | solution.py:519
  141.3 27.3 %collective-permute-start.17 = (bf16[384,1024]{1,0:T(8,128)(2,1)}, bf16[384,1024]{1,0:T(8,128)(2,1)}, u32[]{:S(2)}, u32[]{:S(2)}) collective-permute-start(bf16[384,1024]{1,0:T(8,128)(2,1)} %get-tuple-element.24), channel_id=1, source_target_pairs={{2,0},{3,1},{4,2},{5,3},{6,4},{7,5},{10,8},{11,9},{12,10},{13,11},... | collective-permute-start | bytes 2359304 | tf_op jit(solution)/shard_map/ppermute | solution.py:519
  (12 other events, 35.9 us)
